TPU v7x, 256 devices: a whole 4x4x8 slice. The times are simulated.
256 devices in a mesh: cd: 64 (over y, z, core), ab: 4 (over x).
Axes of the slice: x: 4, y: 4, z: 8, core: 2. Of those that a mesh axis runs over, the one named last changes fastest.
Arguments:
- amplitudes: float32 [2, 128, 458752], P(None, 'ab', 'cd'), may hold values from -16 to 16
- integrals: float32 [458752, 1536], P('cd', 'ab'), may hold values from -0.0078125 to 0.0078125
- c_index: int32 [458752], P('cd'), may hold values from 0 to 1532, as said below
- d_index: int32 [458752], P('cd'), may hold values from 0 to 1535
- a_index: int32 [1536], P('ab'), may hold values from 0 to 1532, as said below
- b_index: int32 [1536], P('ab'), may hold values from 0 to 1535
Outputs:
- ladder: float32 [128, 2, 1536], P('cd', None, 'ab')
Inputs may be any that keep to these rules, and one draw needn't show every extreme that they name: c_index[p] <= d_index[p] for every pair; some pairs have c_index equal to d_index. a_index[q] <= b_index[q] for every result pair; some have a_index equal to b_index.
All inputs are finite; a program needn't handle non-finite values.
Results may differ from a plain program's by a relative error of at most 0.00007.
Values sent between devices are 32-bit elements; how exact they have to be, the bound alone decides.
No kernel may reach another device: no remote copies, remote signals or barrier semaphores. Data moves between devices by JAX's collectives and lax.ppermute only.
A program may use at most 64 MiB of HBM per device.

v0:
```python
import jax
import jax.numpy as jnp
from jax import lax
from jax.sharding import PartitionSpec as P


def contract(block, integrals):
    return jnp.einsum("sip,pq->isq", block, integrals, precision=lax.Precision.HIGHEST)


def local(amplitudes, integrals, c_index, d_index, a_index, b_index):
    same = c_index == d_index
    weight_plus = jnp.where(same, jnp.float32(0.5), jnp.float32(1.0))
    weight_minus = jnp.where(same, jnp.float32(0.0), jnp.float32(1.0))
    weights = jnp.stack([weight_plus, weight_minus])
    weighted = amplitudes * weights[:, None, :]
    part_sum = contract(lax.all_gather(weighted, "ab", axis=1, tiled=True), integrals)
    summed = lax.psum_scatter(part_sum, "cd", scatter_dimension=0, tiled=True)
    keep = jnp.where(a_index == b_index, jnp.float32(0.0), jnp.float32(1.0))
    factor = 0.5 * jnp.stack([jnp.ones_like(keep), keep])
    return summed * factor[None, :, :]


def solution(mesh):
    placed = (P(None, "ab", "cd"), P("cd", "ab"), P("cd"), P("cd"), P("ab"), P("ab"))
    return jax.shard_map(
        local, mesh=mesh, in_specs=placed, out_specs=P("cd", None, "ab"), check_vma=False
    )
```

profile of v0, /device:TPU:32, one launch (start us, length us, event | category | flops | bytes accessed | tf_op | source)
XLA Modules:
  0.0 294.1 jit_solution(12693226184351414701)
XLA Ops:
  6.5 0.0 all-gather.2.cloned.1.call-start
  6.5 0.8 broadcast_select_fusion.1
  7.3 0.1 pad_maximum_fusion
  7.4 3.0 %broadcast_multiply_fusion = f32[2,32,7168]{2,1,0:T(8,128)} fusion(f32[2,32,7168]{2,1,0:T(8,128)} %param.6, f32[2,7168]{1,0:T(2,128)S(1)} %pad_maximum_fusion), kind=kLoop, calls=%fused_computation.3 | loop fusion | flops 458752 | bytes 3727360 | tf_op jit(solution)/shard_map/mul | solution.py:16
  10.3 0.0 all-gather.2.cloned.1.call-update
  10.4 0.0 copy-start
  10.4 0.0 copy-start.1
  10.4 0.0 copy-start.2
  10.4 0.0 all-reduce.4.cloned.1.call-start
  10.5 79.6 %all-gather.2.cloned.1.call-done = f32[2,128,7168]{2,1,0:T(8,128)} async-done(((f32[2,32,7168]{2,1,0:T(8,128)}), f32[2,128,7168]{2,1,0:T(8,128)}) %all-gather.2.cloned.1.call-update) | async-done | bytes 7340048 | tf_op jit(solution)/shard_map/all_gather | solution.py:17
  90.0 16.7 %fusion.2 = f32[128,2,384]{2,0,1:T(8,128)} fusion(f32[2,128,7168]{2,1,0:T(8,128)} %all-gather.2.cloned.1.call-done, f32[7168,384]{1,0:T(8,128)} %param.7), kind=kOutput, calls=%fused_computation.2 | convolution fusion | flops 8455716864 | bytes 18743296 | tf_op jit(solution)/shard_map/sip,pq->isq/dot_general | solution.py:8
  106.7 0.0 all-reduce.4.cloned.1.call-update
  106.8 0.0 copy-done
  106.8 0.0 copy-done.1
  106.8 0.0 copy-done.2
  106.8 0.6 dynamic-slice
  108.1 177.8 %all-reduce.4.cloned.1.call-done = f32[128,2,384]{2,0,1:T(8,128)} async-done(((f32[128,2,384]{2,0,1:T(8,128)}), f32[128,2,384]{2,0,1:T(8,128)}) %all-reduce.4.cloned.1.call-update) | async-done | bytes 393232
  285.9 0.7 dynamic-slice_multiply_fusion
  286.6 0.6 copy.8
  (4 shorter events, 0.0 us)
Async XLA Ops:
  6.5 83.5 %all-gather.2.cloned.1.call-start = ((), (), s32[]{:S(2)}) async-start(), calls=%async_computation | async-start | bytes 9175040 | tf_op jit(solution)/shard_map/all_gather | solution.py:17
  10.4 96.4 %copy-start = (s32[384]{0:T(512)S(1)}, s32[384]{0:T(512)}, u32[]{:S(2)}) copy-start(s32[384]{0:T(512)} %param.10) | copy-start | bytes 4612
  10.4 96.4 %copy-start.1 = (s32[384]{0:T(512)S(1)}, s32[384]{0:T(512)}, u32[]{:S(2)}) copy-start(s32[384]{0:T(512)} %param.11) | copy-start | bytes 4612
  10.4 96.4 %copy-start.2 = (u32[256]{0:T(256)S(1)}, u32[256]{0:T(256)}, u32[]{:S(2)}) copy-start(u32[256]{0:T(256)} %constant.12) | copy-start | bytes 3076
  10.4 275.5 %all-reduce.4.cloned.1.call-start = ((), (), s32[]{:S(2)}) async-start(), calls=%async_computation.1 | async-start | bytes 786432
Sparse Core Ops, SparseCore 0:
  10.5 79.4 all-gather.1
  106.9 178.9 all-reduce.3
where the time goes:
time: 297 us; the launch traced here: 294 us
  waiting for transfers between devices  257 us (87%)
  matrix products  16.7 us (6%)
  between operations  14.1 us (5%)
  other arithmetic  4.55 us (2%)
    unnamed x3, waiting for transfers between devices  178 us
    all_gather x1, waiting for transfers between devices, local(): lax.all_gather(weighted, 'ab', axis=1, tiled=True)  79.6 us
    dot_general x1, matrix products, contract(): jnp.einsum('sip,pq->isq', block, integrals, precision=lax.Precision.HIGHEST)  16.7 us
  transfers between devices with their start and end apart: 2, of which 2 were waited for; matrix products, arithmetic and copies ran while one was open for 0% of the time, Pallas kernels for 0%

commit v1 on v0

v1 whole, which is shorter than its diff:
```python
import functools

import jax
import jax.numpy as jnp
from jax import lax
from jax.experimental import pallas as pl
from jax.experimental.pallas import tpu as pltpu
from jax.sharding import PartitionSpec as P

F32 = jnp.float32
BF16 = jnp.bfloat16
STEP = 1792


def halves(x):
    high = x.astype(BF16)
    return high, (x - high.astype(F32)).astype(BF16)


def products(pieces, block):
    highs, lows = zip(*[halves(piece) for piece in pieces])
    rows = sum(piece.shape[0] for piece in pieces)
    block_high, block_low = halves(block)
    high = jnp.concatenate(highs, axis=0)
    both = jnp.concatenate([high] + list(lows), axis=0)
    first = jnp.dot(both, block_high, preferred_element_type=F32)
    second = jnp.dot(high, block_low, preferred_element_type=F32)
    return first[:rows] + (first[rows:] + second)


def sum_kernel(slabs, *refs):
    piece_refs, (weight_ref, block_ref, total_ref) = refs[: len(slabs)], refs[len(slabs) :]

    @pl.when(pl.program_id(0) == 0)
    def _():
        total_ref[...] = jnp.zeros_like(total_ref)

    pieces = [ref[...] * weight_ref[slab : slab + 1, :] for ref, slab in zip(piece_refs, slabs)]
    total_ref[...] += products(pieces, block_ref[...])


def partial_sums(pieces, slabs, weights, integrals, first_step=0):
    rows = sum(piece.shape[0] for piece in pieces)
    pairs, columns = pieces[0].shape[1], integrals.shape[1]
    return pl.pallas_call(
        functools.partial(sum_kernel, slabs),
        grid=(pairs // STEP,),
        in_specs=[pl.BlockSpec((piece.shape[0], STEP), lambda k: (0, k)) for piece in pieces]
        + [
            pl.BlockSpec((2, STEP), lambda k: (0, k + first_step)),
            pl.BlockSpec((STEP, columns), lambda k: (k + first_step, 0)),
        ],
        out_specs=pl.BlockSpec((rows, columns), lambda k: (0, 0)),
        out_shape=jax.ShapeDtypeStruct((rows, columns), F32),
        compiler_params=pltpu.CompilerParams(vmem_limit_bytes=40 * 2**20),
        cost_estimate=pl.CostEstimate(
            flops=6 * rows * pairs * columns, bytes_accessed=4 * pairs * (rows + columns), transcendentals=0
        ),
    )(*pieces, weights, integrals)


def last_kernel(slabs, *refs):
    n = len(slabs)
    piece_refs, refs = refs[:n], refs[n:]
    weight_ref, block_ref, own_ref, near_ref, far_ref, opposite_ref, out_ref, total_ref = refs
    step = pl.program_id(0)

    @pl.when(step == 0)
    def _():
        total_ref[...] = opposite_ref[...]

    pieces = [ref[...] * weight_ref[slab : slab + 1, :] for ref, slab in zip(piece_refs, slabs)]
    total_ref[...] += products(pieces, block_ref[...])

    @pl.when(step == pl.num_programs(0) - 1)
    def _():
        me = lax.axis_index("ab")
        for ref, first, away, slab in (
            (own_ref, 0, 0, 0),
            (own_ref, 32, 0, 1),
            (near_ref, 0, 3, 0),
            (near_ref, 32, 1, 1),
            (far_ref, 0, 3, 1),
            (far_ref, 32, 1, 0),
            (total_ref, 0, 2, 0),
            (total_ref, 32, 2, 1),
        ):
            group = lax.rem(me + away, 4)
            for pair in range(16):
                out_ref[16 * group + pair, 2 * slab : 2 * slab + 2, :] = ref[first + 2 * pair : first + 2 * pair + 2, :]


def last_sums(pieces, slabs, weights, integrals, first_step, own, near, far, opposite):
    pairs, columns = pieces[0].shape[1], integrals.shape[1]
    whole = pl.BlockSpec((64, columns), lambda k: (0, 0))
    return pl.pallas_call(
        functools.partial(last_kernel, slabs),
        grid=(pairs // STEP,),
        in_specs=[pl.BlockSpec((piece.shape[0], STEP), lambda k: (0, k)) for piece in pieces]
        + [
            pl.BlockSpec((2, STEP), lambda k: (0, k + first_step)),
            pl.BlockSpec((STEP, columns), lambda k: (k + first_step, 0)),
        ]
        + [whole] * 4,
        out_specs=pl.BlockSpec((64, 4, columns), lambda k: (0, 0, 0)),
        out_shape=jax.ShapeDtypeStruct((64, 4, columns), F32),
        scratch_shapes=[pltpu.VMEM((64, columns), F32)],
        compiler_params=pltpu.CompilerParams(vmem_limit_bytes=40 * 2**20),
        cost_estimate=pl.CostEstimate(
            flops=6 * 64 * pairs * columns, bytes_accessed=4 * pairs * (64 + columns), transcendentals=0
        ),
    )(*pieces, weights, integrals, own, near, far, opposite)


def local(amplitudes, integrals, c_index, d_index, a_index, b_index):
    def right(x):
        return lax.ppermute(x, "ab", [(i, (i + 1) % 4) for i in range(4)])

    def left(x):
        return lax.ppermute(x, "ab", [(i, (i - 1) % 4) for i in range(4)])

    pairs, columns = integrals.shape
    half = pairs // 2
    plus, minus = amplitudes[0], amplitudes[1]
    right_plus, left_minus = right(plus), left(minus)
    right_minus, left_plus = right(minus), left(plus)
    onward = [right(right_plus[:, :half]), left(left_minus[:, :half])]
    onward_last = [right(right_plus[:, half:]), left(left_minus[:, half:])]

    same = c_index == d_index
    weights = jnp.stack([jnp.where(same, F32(0.5), F32(1.0)), jnp.where(same, F32(0.0), F32(1.0))])
    own = partial_sums([plus, minus], (0, 1), weights, integrals)
    near = partial_sums([right_plus, left_minus], (0, 1), weights, integrals)
    far = partial_sums([right_minus, left_plus], (1, 0), weights, integrals)
    opposite = partial_sums(onward, (0, 1), weights, integrals)
    part_sum = last_sums(onward_last, (0, 1), weights, integrals, half // STEP, own, near, far, opposite)

    shares = lax.all_to_all(part_sum, "cd", 0, 0, tiled=True)
    summed = jnp.sum(shares.reshape(64, 4, columns), axis=0).reshape(2, 2, columns).transpose(1, 0, 2)
    keep = jnp.where(a_index == b_index, F32(0.0), F32(1.0))
    factor = 0.5 * jnp.stack([jnp.ones_like(keep), keep])
    return summed * factor[None, :, :]


def solution(mesh):
    placed = (P(None, "ab", "cd"), P("cd", "ab"), P("cd"), P("cd"), P("ab"), P("ab"))
    return jax.shard_map(local, mesh=mesh, in_specs=placed, out_specs=P("cd", None, "ab"), check_vma=False)
```

time: 297 us -> 103 us (0.35)
  waiting for transfers between devices: 257 us -> 50.2 us
  starting transfers between devices: 0.04 us -> 21.6 us
  Pallas kernels: 0 us -> 17.9 us
  matrix products: 16.7 us -> 0 us
  between operations: 14.1 us -> 0.19 us
  local copies, waits for them, and re-layouts: 1.2 us -> 11.1 us
  other arithmetic: 4.55 us -> 0.19 us
    unnamed x3 -> x0, waiting for transfers between devices: 178 us -> none
    all_gather x1 -> x0, waiting for transfers between devices: 79.6 us -> none  [local(): lax.all_gather(weighted, 'ab', axis=1, tiled=True)]
    ppermute x0 -> x8, waiting for transfers between devices: none -> 35.8 us  [the longest x4 18.3 us: right(): return lax.ppermute(x, 'ab', [(i, (i + 1) % 4) for i in range(4)])]
    pallas_call x0 -> x5, Pallas kernels: none -> 17.9 us  [the longest x4 14.3 us: partial_sums(): pl.pallas_call(functools.partial(sum_kernel, slabs), grid=(pairs // STEP,...]
    dot_general x1 -> x0, matrix products: 16.7 us -> none  [contract(): jnp.einsum('sip,pq->isq', block, integrals, precision=lax.Precision.HIGHEST)]
    all_to_all x0 -> x1, waiting for transfers between devices: none -> 14.4 us  [local(): shares = lax.all_to_all(part_sum, 'cd', 0, 0, tiled=True)]
    all_to_all x0 -> x1, starting transfers between devices: none -> 11.8 us  [local(): shares = lax.all_to_all(part_sum, 'cd', 0, 0, tiled=True)]
    ppermute x0 -> x8, starting transfers between devices: none -> 9.81 us  [the longest x4 9.79 us: left(): return lax.ppermute(x, 'ab', [(i, (i - 1) % 4) for i in range(4)])]
  transfers between devices with their start and end apart: 2 -> 9, of which waited for: 2 -> 4; matrix products, arithmetic and copies ran while one was open for 0% -> 2% of each run, Pallas kernels for 0% -> 14%
where the time goes in v1:
time: 103 us; the launch traced here: 101 us
  waiting for transfers between devices  50.2 us (49%)
  starting transfers between devices  21.6 us (21%)
  Pallas kernels  17.9 us (17%)
  local copies, waits for them, and re-layouts  11.1 us (11%)
    ppermute x4, waiting for transfers between devices, right(): return lax.ppermute(x, 'ab', [(i, (i + 1) % 4) for i in range(4)])  18.3 us
    ppermute x4, waiting for transfers between devices, left(): return lax.ppermute(x, 'ab', [(i, (i - 1) % 4) for i in range(4)])  17.5 us
    all_to_all x1, waiting for transfers between devices, local(): shares = lax.all_to_all(part_sum, 'cd', 0, 0, tiled=True)  14.4 us
    pallas_call x4, Pallas kernels, partial_sums(): pl.pallas_call(functools.partial(sum_kernel, slabs), grid=(pairs // STEP,...  14.3 us
    all_to_all x1, starting transfers between devices, local(): shares = lax.all_to_all(part_sum, 'cd', 0, 0, tiled=True)  11.8 us
    ppermute x4, starting transfers between devices, left(): return lax.ppermute(x, 'ab', [(i, (i - 1) % 4) for i in range(4)])  9.79 us
    unnamed x20, local copies, waits for them, and re-layouts  6.88 us
    pallas_call x1, Pallas kernels, last_sums(): pl.pallas_call(functools.partial(last_kernel, slabs), grid=(pairs // STEP...  3.59 us
  transfers between devices with their start and end apart: 9, of which 4 were waited for; matrix products, arithmetic and copies ran while one was open for 2% of the time, Pallas kernels for 14%

profile of v1, /device:TPU:32, one launch (start us, length us, event | category | flops | bytes accessed | tf_op | source)
XLA Modules:
  0.0 101.1 jit_solution(1634569980425848232)
XLA Ops:
  0.0 1.6 %slice_bitcast_fusion = (f32[32,7168]{1,0:T(8,128)S(1)}, f32[32,7168]{1,0:T(8,128)S(1)}) fusion(f32[2,32,7168]{2,1,0:T(8,128)} %param.6), kind=kLoop, calls=%fused_computation | loop fusion | bytes 3670016 | tf_op jit(solution)/shard_map/squeeze | solution.py:124
  1.6 2.8 %collective-permute-start.2 = (f32[32,7168]{1,0:T(8,128)S(1)}, f32[32,7168]{1,0:T(8,128)S(1)}, u32[]{:S(2)}, u32[]{:S(2)}) collective-permute-start(f32[32,7168]{1,0:T(8,128)S(1)} %get-tuple-element.7.refs_1_), channel_id=1, source_target_pairs={{0,3},{1,0},{2,1},{3,2},{4,7},{5,4},{6,5},{7,6},{8,11},{9,8},{10,9... | collective-permute-start | bytes 2752520 | tf_op jit(solution)/shard_map/ppermute | solution.py:120
  4.4 0.0 collective-permute-start.4
  4.4 3.2 %collective-permute-start.5 = (f32[32,7168]{1,0:T(8,128)S(1)}, f32[32,7168]{1,0:T(8,128)}, u32[]{:S(2)}, u32[]{:S(2)}) collective-permute-start(f32[32,7168]{1,0:T(8,128)S(1)} %get-tuple-element.8.refs_0_), channel_id=1, source_target_pairs={{0,3},{1,0},{2,1},{3,2},{4,7},{5,4},{6,5},{7,6},{8,11},{9,8},{10,9... | collective-permute-start | bytes 2752520 | tf_op jit(solution)/shard_map/ppermute | solution.py:120
  7.7 0.0 collective-permute-start
  7.7 17.5 %collective-permute-done.2.refs_1_ = f32[32,7168]{1,0:T(8,128)S(1)} collective-permute-done((f32[32,7168]{1,0:T(8,128)S(1)}, f32[32,7168]{1,0:T(8,128)S(1)}, u32[]{:S(2)}, u32[]{:S(2)}) %collective-permute-start.2) | collective-permute-done | bytes 917536 | tf_op jit(solution)/shard_map/ppermute | solution.py:120
  25.2 1.0 fusion
  26.2 3.7 %collective-permute-start.7 = (f32[32,3584]{1,0:T(8,128)}, f32[32,3584]{1,0:T(8,128)}, u32[]{:S(2)}, u32[]{:S(2)}) collective-permute-start(f32[32,3584]{1,0:T(8,128)} %get-tuple-element.9), channel_id=1, source_target_pairs={{0,3},{1,0},{2,1},{3,2},{4,7},{5,4},{6,5},{7,6},{8,11},{9,8},{10,9... | collective-permute-start | bytes 1376264 | tf_op jit(solution)/shard_map/ppermute | solution.py:120
  29.9 0.0 collective-permute-start.3
  29.9 17.2 %collective-permute-done.refs_0_ = f32[32,7168]{1,0:T(8,128)S(1)} collective-permute-done((f32[32,7168]{1,0:T(8,128)S(1)}, f32[32,7168]{1,0:T(8,128)S(1)}, u32[]{:S(2)}, u32[]{:S(2)}) %collective-permute-start) | collective-permute-done | bytes 917536 | tf_op jit(solution)/shard_map/ppermute | solution.py:117
  47.1 1.1 %fusion.1 = (f32[32,3584]{1,0:T(8,128)}, f32[32,3584]{1,0:T(8,128)}) fusion(f32[32,7168]{1,0:T(8,128)S(1)} %collective-permute-done.refs_0_), kind=kLoop, calls=%fused_computation.9 | loop fusion | bytes 1835008 | tf_op jit(solution)/shard_map/slice | solution.py:127
  48.2 0.0 collective-permute-start.6
  48.2 0.0 collective-permute-done.4.refs_0_
  48.2 0.9 copy-done.4
  49.1 0.1 pad_maximum_fusion.refs_2_
  49.2 0.0 copy-start
  49.2 4.1 %copy-done = f32[7168,384]{1,0:T(8,128)S(1)} copy-done((f32[7168,384]{1,0:T(8,128)S(1)}, f32[7168,384]{1,0:T(8,128)}, u32[]{:S(2)}) %copy-start) | copy-done | bytes 11010072
  53.3 3.5 %shard_map.64.refs_4_ = f32[64,384]{1,0:T(8,128)S(1)} custom-call(f32[32,7168]{1,0:T(8,128)S(1)} %get-tuple-element.8.refs_0_, f32[32,7168]{1,0:T(8,128)S(1)} %get-tuple-element.7.refs_1_, f32[2,7168]{1,0:T(2,128)S(1)} %pad_maximum_fusion.refs_2_, f32[7168,384]{1,0:T(8,128)S(1)} %copy-done), custom_call_target="tpu_custom_call" | custom-call | flops 1056964608 | bytes 12845056 | tf_op jit(solution)/shard_map/pallas_call | solution.py:45
  56.8 0.6 copy-done.1
  57.4 1.2 %copy-done.3 = f32[32,7168]{1,0:T(8,128)S(1)} copy-done((f32[32,7168]{1,0:T(8,128)S(1)}, f32[32,7168]{1,0:T(8,128)}, u32[]{:S(2)}) %copy-start.3) | copy-done | bytes 917528
  58.6 3.5 %shard_map.65.refs_5_ = f32[64,384]{1,0:T(8,128)S(1)} custom-call(f32[32,7168]{1,0:T(8,128)S(1)} %copy-done.3, f32[32,7168]{1,0:T(8,128)S(1)} %collective-permute-done.2.refs_1_, f32[2,7168]{1,0:T(2,128)S(1)} %pad_maximum_fusion.refs_2_, f32[7168,384]{1,0:T(8,128)S(1)} %copy-done.1), custom_call_target="tpu_custom_call" | custom-call | flops 1056964608 | bytes 12845056 | tf_op jit(solution)/shard_map/pallas_call | solution.py:45
  62.2 4.5 %shard_map.66.refs_6_ = f32[64,384]{1,0:T(8,128)S(1)} custom-call(f32[32,7168]{1,0:T(8,128)S(1)} %copy-done.5, f32[32,7168]{1,0:T(8,128)} %collective-permute-done.5.refs_1_, f32[2,7168]{1,0:T(2,128)S(1)} %pad_maximum_fusion.refs_2_, f32[7168,384]{1,0:T(8,128)S(1)} %copy-done.1), custom_call_target="tpu_custom_call" | custom-call | flops 1056964608 | bytes 12845056 | tf_op jit(solution)/shard_map/pallas_call | solution.py:45
  66.7 0.0 collective-permute-done.7.refs_1_
  66.7 2.7 %shard_map.67.refs_7_ = f32[64,384]{1,0:T(8,128)S(1)} custom-call(f32[32,3584]{1,0:T(8,128)} %collective-permute-done.6.refs_0_, f32[32,3584]{1,0:T(8,128)} %collective-permute-done.7.refs_1_, f32[2,7168]{1,0:T(2,128)S(1)} %pad_maximum_fusion.refs_2_, f32[7168,384]{1,0:T(8,128)S(1)} %copy-done.1), custom_call_target="tpu_custom_call" | custom-call | flops 528482304 | bytes 6422528 | tf_op jit(solution)/shard_map/pallas_call | solution.py:45
  69.4 0.0 copy-start.8
  69.5 0.0 copy-start.9
  69.5 1.1 %collective-permute-done.1.refs_0_ = f32[32,3584]{1,0:T(8,128)} collective-permute-done((f32[32,3584]{1,0:T(8,128)}, f32[32,3584]{1,0:T(8,128)}, u32[]{:S(2)}, u32[]{:S(2)}) %collective-permute-start.1) | collective-permute-done | bytes 458784 | tf_op jit(solution)/shard_map/ppermute | solution.py:117
  70.6 3.6 %shard_map.68 = f32[64,4,384]{2,1,0:T(4,128)} custom-call(f32[32,3584]{1,0:T(8,128)} %collective-permute-done.1.refs_0_, f32[32,3584]{1,0:T(8,128)} %collective-permute-done.3.refs_1_, f32[2,7168]{1,0:T(2,128)S(1)} %pad_maximum_fusion.refs_2_, f32[7168,384]{1,0:T(8,128)S(1)} %copy-done.1, f32[64,384]{1,0:T(8,128)S(1)} %shard_map.64.refs_4_, ...), custom_call_target="tpu_custom_call" | custom-call | flops 528482304 | bytes 6422528 | tf_op jit(solution)/shard_map/pallas_call | solution.py:96
  74.2 11.8 %all-to-all-start = ((f32[64,4,384]{2,1,0:T(4,128)}), f32[64,4,384]{2,1,0:T(4,128)S(1)}, u32[]{:S(2)}, u32[]{:S(2)}) async-start(f32[64,4,384]{2,1,0:T(4,128)} %shard_map.68), calls=%async_computation | async-start | bytes 786432 | tf_op jit(solution)/shard_map/all_to_all | solution.py:138
  86.0 14.4 %all-to-all-done = f32[64,4,384]{2,1,0:T(4,128)S(1)} async-done(((f32[64,4,384]{2,1,0:T(4,128)}), f32[64,4,384]{2,1,0:T(4,128)S(1)}, u32[]{:S(2)}, u32[]{:S(2)}) %all-to-all-start) | async-done | bytes 393248 | tf_op jit(solution)/shard_map/all_to_all | solution.py:138
  100.4 0.1 reduce_sum.9
  100.5 0.6 copy.7
  (24 shorter events, 0.1 us)
Async XLA Ops:
  0.0 7.7 %copy-start.7 = (s32[7168]{0:T(1024)S(1)}, s32[7168]{0:T(1024)}, u32[]{:S(2)}) copy-start(s32[7168]{0:T(1024)} %param.9) | copy-start | bytes 86020
  0.0 7.7 %copy-start.6 = (s32[7168]{0:T(1024)S(1)}, s32[7168]{0:T(1024)}, u32[]{:S(2)}) copy-start(s32[7168]{0:T(1024)} %param.8) | copy-start | bytes 86020
  1.6 23.6 %collective-permute-start.2 = (f32[32,7168]{1,0:T(8,128)S(1)}, f32[32,7168]{1,0:T(8,128)S(1)}, u32[]{:S(2)}, u32[]{:S(2)}) collective-permute-start(f32[32,7168]{1,0:T(8,128)S(1)} %get-tuple-element.7.refs_1_), channel_id=1, source_target_pairs={{0,3},{1,0},{2,1},{3,2},{4,7},{5,4},{6,5},{7,6},{8,11},{9,8},{10,9... | collective-permute-start | bytes 2752520 | tf_op jit(solution)/shard_map/ppermute | solution.py:120
  4.4 43.7 %collective-permute-start.4 = (f32[32,7168]{1,0:T(8,128)S(1)}, f32[32,7168]{1,0:T(8,128)S(1)}, u32[]{:S(2)}, u32[]{:S(2)}) collective-permute-start(f32[32,7168]{1,0:T(8,128)S(1)} %get-tuple-element.7.refs_1_), channel_id=1, source_target_pairs={{0,1},{1,2},{2,3},{3,0},{4,5},{5,6},{6,7},{7,4},{8,9},{9,10},{10,1... | collective-permute-start | bytes 2752520 | tf_op jit(solution)/shard_map/ppermute | solution.py:117
  4.4 57.7 %collective-permute-start.5 = (f32[32,7168]{1,0:T(8,128)S(1)}, f32[32,7168]{1,0:T(8,128)}, u32[]{:S(2)}, u32[]{:S(2)}) collective-permute-start(f32[32,7168]{1,0:T(8,128)S(1)} %get-tuple-element.8.refs_0_), channel_id=1, source_target_pairs={{0,3},{1,0},{2,1},{3,2},{4,7},{5,4},{6,5},{7,6},{8,11},{9,8},{10,9... | collective-permute-start | bytes 2752520 | tf_op jit(solution)/shard_map/ppermute | solution.py:120
  7.7 39.4 %collective-permute-start = (f32[32,7168]{1,0:T(8,128)S(1)}, f32[32,7168]{1,0:T(8,128)S(1)}, u32[]{:S(2)}, u32[]{:S(2)}) collective-permute-start(f32[32,7168]{1,0:T(8,128)S(1)} %get-tuple-element.8.refs_0_), channel_id=1, source_target_pairs={{0,1},{1,2},{2,3},{3,0},{4,5},{5,6},{6,7},{7,4},{8,9},{9,10},{10,1... | collective-permute-start | bytes 2752520 | tf_op jit(solution)/shard_map/ppermute | solution.py:117
  26.2 40.5 %collective-permute-start.7 = (f32[32,3584]{1,0:T(8,128)}, f32[32,3584]{1,0:T(8,128)}, u32[]{:S(2)}, u32[]{:S(2)}) collective-permute-start(f32[32,3584]{1,0:T(8,128)} %get-tuple-element.9), channel_id=1, source_target_pairs={{0,3},{1,0},{2,1},{3,2},{4,7},{5,4},{6,5},{7,6},{8,11},{9,8},{10,9... | collective-permute-start | bytes 1376264 | tf_op jit(solution)/shard_map/ppermute | solution.py:120
  29.9 39.6 %collective-permute-start.3 = (f32[32,3584]{1,0:T(8,128)}, f32[32,3584]{1,0:T(8,128)}, u32[]{:S(2)}, u32[]{:S(2)}) collective-permute-start(f32[32,3584]{1,0:T(8,128)} %get-tuple-element.10), channel_id=1, source_target_pairs={{0,3},{1,0},{2,1},{3,2},{4,7},{5,4},{6,5},{7,6},{8,11},{9,8},{10,9... | collective-permute-start | bytes 1376264 | tf_op jit(solution)/shard_map/ppermute | solution.py:120
  47.1 2.0 %copy-start.2 = (f32[32,7168]{1,0:T(8,128)}, f32[32,7168]{1,0:T(8,128)S(1)}, u32[]{:S(2)}) copy-start(f32[32,7168]{1,0:T(8,128)S(1)} %collective-permute-done.refs_0_) | copy-start | bytes 2752516
  48.2 18.5 %collective-permute-start.6 = (f32[32,3584]{1,0:T(8,128)}, f32[32,3584]{1,0:T(8,128)}, u32[]{:S(2)}, u32[]{:S(2)}) collective-permute-start(f32[32,3584]{1,0:T(8,128)} %get-tuple-element.11), channel_id=1, source_target_pairs={{0,1},{1,2},{2,3},{3,0},{4,5},{5,6},{6,7},{7,4},{8,9},{9,10},{10,1... | collective-permute-start | bytes 1376264 | tf_op jit(solution)/shard_map/ppermute | solution.py:117
  48.2 0.9 copy-start.4
  49.1 21.5 %collective-permute-start.1 = (f32[32,3584]{1,0:T(8,128)}, f32[32,3584]{1,0:T(8,128)}, u32[]{:S(2)}, u32[]{:S(2)}) collective-permute-start(f32[32,3584]{1,0:T(8,128)} %get-tuple-element.12), channel_id=1, source_target_pairs={{0,1},{1,2},{2,3},{3,0},{4,5},{5,6},{6,7},{7,4},{8,9},{9,10},{10,1... | collective-permute-start | bytes 1376264 | tf_op jit(solution)/shard_map/ppermute | solution.py:117
  49.2 4.1 %copy-start = (f32[7168,384]{1,0:T(8,128)S(1)}, f32[7168,384]{1,0:T(8,128)}, u32[]{:S(2)}) copy-start(f32[7168,384]{1,0:T(8,128)} %refs_3_.9) | copy-start | bytes 33030148
  53.3 4.1 %copy-start.1 = (f32[7168,384]{1,0:T(8,128)S(1)}, f32[7168,384]{1,0:T(8,128)}, u32[]{:S(2)}) copy-start(f32[7168,384]{1,0:T(8,128)} %refs_3_.9) | copy-start | bytes 33030148
  57.4 1.2 %copy-start.3 = (f32[32,7168]{1,0:T(8,128)S(1)}, f32[32,7168]{1,0:T(8,128)}, u32[]{:S(2)}) copy-start(f32[32,7168]{1,0:T(8,128)} %copy-done.2) | copy-start | bytes 2752516
  58.6 3.5 %copy-start.5 = (f32[32,7168]{1,0:T(8,128)S(1)}, f32[32,7168]{1,0:T(8,128)}, u32[]{:S(2)}) copy-start(f32[32,7168]{1,0:T(8,128)} %copy-done.4) | copy-start | bytes 2752516
  69.4 16.5 %copy-start.8 = (s32[384]{0:T(512)S(1)}, s32[384]{0:T(512)}, u32[]{:S(2)}) copy-start(s32[384]{0:T(512)} %param.10) | copy-start | bytes 4612
  69.5 16.5 %copy-start.9 = (s32[384]{0:T(512)S(1)}, s32[384]{0:T(512)}, u32[]{:S(2)}) copy-start(s32[384]{0:T(512)} %param.11) | copy-start | bytes 4612
  74.2 26.2 %all-to-all-start = ((f32[64,4,384]{2,1,0:T(4,128)}), f32[64,4,384]{2,1,0:T(4,128)S(1)}, u32[]{:S(2)}, u32[]{:S(2)}) async-start(f32[64,4,384]{2,1,0:T(4,128)} %shard_map.68), calls=%async_computation | async-start | bytes 786432 | tf_op jit(solution)/shard_map/all_to_all | solution.py:138

commit v2 on v0

v2 whole, which is shorter than its diff:
```python
import functools

import jax
import jax.numpy as jnp
from jax import lax
from jax.experimental import pallas as pl
from jax.experimental.pallas import tpu as pltpu
from jax.sharding import PartitionSpec as P

F32 = jnp.float32
BF16 = jnp.bfloat16
STEP = 1792
VMEM = pltpu.CompilerParams(vmem_limit_bytes=24 * 2**20)
FREE = pl.CostEstimate(flops=0, bytes_accessed=0, transcendentals=0)
GROUPS, LAYERS, CORES = 4, 8, 2


def halves(x):
    high = x.astype(BF16)
    return high, (x - high.astype(F32)).astype(BF16)


def products(rows, block):
    count = rows.shape[0]
    high, low = halves(rows)
    block_high, block_low = halves(block)
    first = jnp.dot(jnp.concatenate([high, low], axis=0), block_high, preferred_element_type=F32)
    return first[:count] + (first[count:] + jnp.dot(high, block_low, preferred_element_type=F32))


def add_step(slabs, piece_refs, weight_ref, block_ref, total_ref):
    rows = [
        ref[...].reshape(-1, ref.shape[-1]) * weight_ref[slab : slab + 1, :] for ref, slab in zip(piece_refs, slabs)
    ]
    total_ref[...] += products(jnp.concatenate(rows, axis=0), block_ref[...])


def sum_kernel(slabs, *refs):
    n = len(slabs)
    total_ref = refs[n + 2]

    @pl.when(pl.program_id(0) == 0)
    def _():
        total_ref[...] = jnp.zeros_like(total_ref)

    add_step(slabs, refs[:n], refs[n], refs[n + 1], total_ref)


def specs(piece_specs, columns, first):
    return piece_specs + [
        pl.BlockSpec((2, STEP), lambda k: (0, k + first)),
        pl.BlockSpec((STEP, columns), lambda k: (k + first, 0)),
    ]


def own_sums(amplitudes, weights, integrals):
    slabs, rows, pairs = amplitudes.shape
    columns = integrals.shape[1]
    own = [pl.BlockSpec((1, rows, STEP), lambda k, s=s: (s, 0, k)) for s in range(slabs)]
    return pl.pallas_call(
        functools.partial(sum_kernel, (0, 1)),
        grid=(pairs // STEP,),
        in_specs=specs(own, columns, 0),
        out_specs=pl.BlockSpec((slabs * rows, columns), lambda k: (0, 0)),
        out_shape=jax.ShapeDtypeStruct((slabs * rows, columns), F32),
        compiler_params=VMEM,
        cost_estimate=FREE,
    )(amplitudes, amplitudes, weights, integrals)


def partial_sums(pieces, slabs, weights, integrals, first=0):
    n, (rows, pairs) = len(pieces), pieces[0].shape
    columns = integrals.shape[1]
    return pl.pallas_call(
        functools.partial(sum_kernel, slabs),
        grid=(pairs // STEP,),
        in_specs=specs([pl.BlockSpec((rows, STEP), lambda k: (0, k))] * n, columns, first),
        out_specs=pl.BlockSpec((n * rows, columns), lambda k: (0, 0)),
        out_shape=jax.ShapeDtypeStruct((n * rows, columns), F32),
        compiler_params=VMEM,
        cost_estimate=FREE,
    )(*pieces, weights, integrals)


def last_kernel(slabs, *refs):
    n = len(slabs)
    own_ref, near_ref, far_ref, opposite_ref, mine_ref, other_ref, total_ref = refs[n + 2 :]
    step = pl.program_id(0)

    @pl.when(step == 0)
    def _():
        total_ref[...] = opposite_ref[...]

    add_step(slabs, refs[:n], refs[n], refs[n + 1], total_ref)

    @pl.when(step == pl.num_programs(0) - 1)
    def _():
        me, core = lax.axis_index("ab"), lax.rem(lax.axis_index("cd"), CORES)
        for ref, start, away, slab in (
            (own_ref, 0, 0, 0),
            (own_ref, 32, 0, 1),
            (near_ref, 0, 3, 0),
            (near_ref, 32, 1, 1),
            (far_ref, 0, 3, 1),
            (far_ref, 32, 1, 0),
            (total_ref, 0, 2, 0),
            (total_ref, 32, 2, 1),
        ):
            group = lax.rem(me + away, GROUPS)
            for layer in range(LAYERS):
                pair = start + 2 * CORES * layer
                first, second = ref[pair : pair + 2, :], ref[pair + 2 : pair + 4, :]
                at = LAYERS * group + layer, slice(2 * slab, 2 * slab + 2)
                mine_ref[at] = jnp.where(core == 0, first, second)
                other_ref[at] = jnp.where(core == 0, second, first)


def last_sums(pieces, slabs, weights, integrals, first, own, near, far, opposite):
    n, (rows, pairs) = len(pieces), pieces[0].shape
    columns = integrals.shape[1]
    whole = [pl.BlockSpec(x.shape, lambda k: (0, 0)) for x in (own, near, far, opposite)]
    return pl.pallas_call(
        functools.partial(last_kernel, slabs),
        grid=(pairs // STEP,),
        in_specs=specs([pl.BlockSpec((rows, STEP), lambda k: (0, k))] * n, columns, first) + whole,
        out_specs=[pl.BlockSpec((GROUPS * LAYERS, 4, columns), lambda k: (0, 0, 0))] * 2,
        out_shape=[jax.ShapeDtypeStruct((GROUPS * LAYERS, 4, columns), F32)] * 2,
        scratch_shapes=[pltpu.VMEM((n * rows, columns), F32)],
        compiler_params=VMEM,
        cost_estimate=FREE,
    )(*pieces, weights, integrals, own, near, far, opposite)


def finish_kernel(shares_ref, a_ref, b_ref, out_ref):
    keep = jnp.where(a_ref[...] == b_ref[...], F32(0.0), F32(0.5))
    summed = jnp.sum(shares_ref[...], axis=0)
    out_ref[:, 0, :] = 0.5 * summed[0:2]
    out_ref[:, 1, :] = keep * summed[2:4]


def pieces_kernel(own_ref, *refs):
    plus_ref, minus_ref = refs[-2:]
    plus_ref[...] = own_ref[0]
    minus_ref[...] = own_ref[1]


def slabs_after(amplitudes, *after):
    _, rows, pairs = amplitudes.shape
    return pl.pallas_call(
        pieces_kernel,
        grid=(pairs // STEP,),
        in_specs=[pl.BlockSpec((2, rows, STEP), lambda k: (0, 0, k))] + [pl.BlockSpec(memory_space=pl.ANY)] * len(after),
        out_specs=[pl.BlockSpec((rows, STEP), lambda k: (0, k))] * 2,
        out_shape=[jax.ShapeDtypeStruct((rows, pairs), F32)] * 2,
        compiler_params=VMEM,
        cost_estimate=FREE,
    )(amplitudes, *after)


def right(x):
    return lax.ppermute(x, "ab", [(i, (i + 1) % GROUPS) for i in range(GROUPS)])


def left(x):
    return lax.ppermute(x, "ab", [(i, (i - 1) % GROUPS) for i in range(GROUPS)])


def over_cores(x):
    return lax.ppermute(x, "cd", [(i, i ^ 1) for i in range(GROUPS * LAYERS * CORES)])


def local(amplitudes, integrals, c_index, d_index, a_index, b_index):
    pairs, columns = integrals.shape
    cut = pairs // 4 * 3

    same = c_index == d_index
    weights = jnp.stack([jnp.where(same, F32(0.5), F32(1.0)), jnp.where(same, F32(0.0), F32(1.0))])

    right_plus, left_minus = right(amplitudes[0]), left(amplitudes[1])
    own = own_sums(amplitudes, weights, integrals)
    plus, minus = slabs_after(amplitudes, own)
    right_minus, left_plus = right(minus), left(plus)
    onward = [right(right_plus[:, :cut]), left(left_minus[:, :cut])]
    onward_last = [right(right_plus[:, cut:]), left(left_minus[:, cut:])]
    near = partial_sums([right_plus, left_minus], (0, 1), weights, integrals)
    far = partial_sums([right_minus, left_plus], (1, 0), weights, integrals)
    opposite = partial_sums(onward, (0, 1), weights, integrals)
    mine, other = last_sums(onward_last, (0, 1), weights, integrals, cut // STEP, own, near, far, opposite)

    both_cores = mine + over_cores(other)
    planes = [[2 * i + core for i in range(GROUPS * LAYERS)] for core in range(CORES)]
    shares = lax.all_to_all(both_cores, "cd", 0, 0, tiled=True, axis_index_groups=planes)
    return pl.pallas_call(
        finish_kernel, out_shape=jax.ShapeDtypeStruct((2, 2, columns), F32), compiler_params=VMEM, cost_estimate=FREE
    )(shares, a_index.reshape(1, columns), b_index.reshape(1, columns))


def solution(mesh):
    placed = (P(None, "ab", "cd"), P("cd", "ab"), P("cd"), P("cd"), P("ab"), P("ab"))
    return jax.shard_map(local, mesh=mesh, in_specs=placed, out_specs=P("cd", None, "ab"), check_vma=False)
```

time: 297 us -> 93.6 us (0.32)
  waiting for transfers between devices: 257 us -> 46.3 us
  starting transfers between devices: 0.04 us -> 24.8 us
  matrix products: 16.7 us -> 0 us
  Pallas kernels: 0 us -> 15.2 us
  between operations: 14.1 us -> 0.22 us
  local copies, waits for them, and re-layouts: 1.2 us -> 6 us
  other arithmetic: 4.55 us -> 0.79 us
    unnamed x3 -> x0, waiting for transfers between devices: 178 us -> none
    all_gather x1 -> x0, waiting for transfers between devices: 79.6 us -> none  [local(): lax.all_gather(weighted, 'ab', axis=1, tiled=True)]
    ppermute x0 -> x9, waiting for transfers between devices: none -> 35.1 us  [the longest x4 20.6 us: right(): return lax.ppermute(x, 'ab', [(i, (i + 1) % GROUPS) for i in range(GROUPS)])]
    dot_general x1 -> x0, matrix products: 16.7 us -> none  [contract(): jnp.einsum('sip,pq->isq', block, integrals, precision=lax.Precision.HIGHEST)]
    pallas_call x0 -> x7, Pallas kernels: none -> 15.2 us  [the longest x3 9.67 us: partial_sums(): pl.pallas_call(functools.partial(sum_kernel, slabs), grid=(pairs // STEP,...]
    ppermute x0 -> x9, starting transfers between devices: none -> 13.5 us  [the longest x4 12.5 us: left(): return lax.ppermute(x, 'ab', [(i, (i - 1) % GROUPS) for i in range(GROUPS)])]
    all_to_all x0 -> x1, starting transfers between devices: none -> 11.4 us  [local(): lax.all_to_all(both_cores, 'cd', 0, 0, tiled=True, axis_index_groups=planes)]
    all_to_all x0 -> x1, waiting for transfers between devices: none -> 11.3 us  [local(): lax.all_to_all(both_cores, 'cd', 0, 0, tiled=True, axis_index_groups=planes)]
  transfers between devices with their start and end apart: 2 -> 10, of which waited for: 2 -> 7; matrix products, arithmetic and copies ran while one was open for 0% -> 0% of each run, Pallas kernels for 0% -> 15%
where the time goes in v2:
time: 93.6 us; the launch traced here: 93.4 us
  waiting for transfers between devices  46.3 us (49%)
  starting transfers between devices  24.8 us (26%)
  Pallas kernels  15.2 us (16%)
  local copies, waits for them, and re-layouts  6 us (6%)
    ppermute x4, waiting for transfers between devices, right(): return lax.ppermute(x, 'ab', [(i, (i + 1) % GROUPS) for i in range(GROUPS)])  20.6 us
    ppermute x4, waiting for transfers between devices, left(): return lax.ppermute(x, 'ab', [(i, (i - 1) % GROUPS) for i in range(GROUPS)])  13.1 us
    ppermute x4, starting transfers between devices, left(): return lax.ppermute(x, 'ab', [(i, (i - 1) % GROUPS) for i in range(GROUPS)])  12.5 us
    all_to_all x1, starting transfers between devices, local(): lax.all_to_all(both_cores, 'cd', 0, 0, tiled=True, axis_index_groups=planes)  11.4 us
    all_to_all x1, waiting for transfers between devices, local(): lax.all_to_all(both_cores, 'cd', 0, 0, tiled=True, axis_index_groups=planes)  11.3 us
    pallas_call x3, Pallas kernels, partial_sums(): pl.pallas_call(functools.partial(sum_kernel, slabs), grid=(pairs // STEP,...  9.67 us
    unnamed x14, local copies, waits for them, and re-layouts  4.15 us
    pallas_call x1, Pallas kernels, own_sums(): pl.pallas_call(functools.partial(sum_kernel, (0, 1)), grid=(pairs // STEP...  3.51 us
  transfers between devices with their start and end apart: 10, of which 7 were waited for; matrix products, arithmetic and copies ran while one was open for 0% of the time, Pallas kernels for 15%

profile of v2, /device:TPU:32, one launch (start us, length us, event | category | flops | bytes accessed | tf_op | source)
XLA Modules:
  0.0 93.4 jit_solution(13927371508616591443)
XLA Ops:
  0.0 1.7 %slice_bitcast_fusion = (f32[32,7168]{1,0:T(8,128)S(1)}, f32[32,7168]{1,0:T(8,128)S(1)}) fusion(f32[2,32,7168]{2,1,0:T(8,128)} %own_ref.1), kind=kLoop, calls=%fused_computation | loop fusion | bytes 3670016 | tf_op jit(solution)/shard_map/squeeze | solution.py:179
  1.7 2.8 %collective-permute-start.2 = (f32[32,7168]{1,0:T(8,128)S(1)}, f32[32,7168]{1,0:T(8,128)S(1)}, u32[]{:S(2)}, u32[]{:S(2)}) collective-permute-start(f32[32,7168]{1,0:T(8,128)S(1)} %get-tuple-element.15), channel_id=1, source_target_pairs={{0,3},{1,0},{2,1},{3,2},{4,7},{5,4},{6,5},{7,6},{8,11},{9,8},{10,9... | collective-permute-start | bytes 2752520 | tf_op jit(solution)/shard_map/ppermute | solution.py:165
  4.6 0.0 collective-permute-start
  4.6 0.1 pad_maximum_fusion.refs_2_
  4.7 0.0 copy-start
  4.7 4.1 %copy-done = f32[7168,384]{1,0:T(8,128)S(1)} copy-done((f32[7168,384]{1,0:T(8,128)S(1)}, f32[7168,384]{1,0:T(8,128)}, u32[]{:S(2)}) %copy-start) | copy-done | bytes 11010072
  8.8 3.5 %shard_map.64.refs_0_.refs_4_ = f32[64,384]{1,0:T(8,128)S(1)} custom-call(f32[2,32,7168]{2,1,0:T(8,128)S(1)} %copy-done.2, f32[2,32,7168]{2,1,0:T(8,128)S(1)} %copy-done.2, f32[2,7168]{1,0:T(2,128)S(1)} %pad_maximum_fusion.refs_2_, f32[7168,384]{1,0:T(8,128)S(1)} %copy-done), custom_call_target="tpu_custom_call" | custom-call | tf_op jit(solution)/shard_map/pallas_call | solution.py:60
  12.3 0.5 shard_map.66
  12.8 0.8 collective-permute-start.4
  13.6 2.6 %collective-permute-start.5 = (f32[32,7168]{1,0:T(8,128)S(1)}, f32[32,7168]{1,0:T(8,128)S(1)}, u32[]{:S(2)}, u32[]{:S(2)}) collective-permute-start(f32[32,7168]{1,0:T(8,128)S(1)} %get-tuple-element.10), channel_id=1, source_target_pairs={{0,3},{1,0},{2,1},{3,2},{4,7},{5,4},{6,5},{7,6},{8,11},{9,8},{10,9... | collective-permute-start | bytes 2752520 | tf_op jit(solution)/shard_map/ppermute | solution.py:165
  16.2 9.1 %collective-permute-done.2.refs_1_ = f32[32,7168]{1,0:T(8,128)S(1)} collective-permute-done((f32[32,7168]{1,0:T(8,128)S(1)}, f32[32,7168]{1,0:T(8,128)S(1)}, u32[]{:S(2)}, u32[]{:S(2)}) %collective-permute-start.2) | collective-permute-done | bytes 917536 | tf_op jit(solution)/shard_map/ppermute | solution.py:165
  25.4 3.8 %collective-permute-start.7 = (f32[32,5376]{1,0:T(8,128)S(1)}, f32[32,5376]{1,0:T(8,128)S(1)}, u32[]{:S(2)}, u32[]{:S(2)}) collective-permute-start(f32[32,5376]{1,0:T(8,128)S(1)} %slice.27), channel_id=1, source_target_pairs={{0,3},{1,0},{2,1},{3,2},{4,7},{5,4},{6,5},{7,6},{8,11},{9,8},{10,9... | collective-permute-start | bytes 2064392 | tf_op jit(solution)/shard_map/ppermute | solution.py:165
  29.2 0.1 collective-permute-start.6
  29.3 3.3 %collective-permute-start.3 = (f32[32,1792]{1,0:T(8,128)S(1)}, f32[32,1792]{1,0:T(8,128)S(1)}, u32[]{:S(2)}, u32[]{:S(2)}) collective-permute-start(f32[32,1792]{1,0:T(8,128)S(1)} %slice.25), channel_id=1, source_target_pairs={{0,3},{1,0},{2,1},{3,2},{4,7},{5,4},{6,5},{7,6},{8,11},{9,8},{10,9... | collective-permute-start | bytes 688136 | tf_op jit(solution)/shard_map/ppermute | solution.py:165
  32.6 16.1 %collective-permute-done.4.refs_0_ = f32[32,7168]{1,0:T(8,128)S(1)} collective-permute-done((f32[32,7168]{1,0:T(8,128)S(1)}, f32[32,7168]{1,0:T(8,128)S(1)}, u32[]{:S(2)}, u32[]{:S(2)}) %collective-permute-start.4) | collective-permute-done | bytes 917536 | tf_op jit(solution)/shard_map/ppermute | solution.py:161
  48.7 0.0 collective-permute-start.1
  48.7 3.5 %shard_map.65.refs_5_ = f32[64,384]{1,0:T(8,128)S(1)} custom-call(f32[32,7168]{1,0:T(8,128)S(1)} %collective-permute-done.refs_0_, f32[32,7168]{1,0:T(8,128)S(1)} %collective-permute-done.2.refs_1_, f32[2,7168]{1,0:T(2,128)S(1)} %pad_maximum_fusion.refs_2_, f32[7168,384]{1,0:T(8,128)S(1)} %copy-done.1), custom_call_target="tpu_custom_call" | custom-call | tf_op jit(solution)/shard_map/pallas_call | solution.py:74
  52.2 0.0 collective-permute-done.5.refs_1_
  52.3 3.5 %shard_map.67.refs_6_ = f32[64,384]{1,0:T(8,128)S(1)} custom-call(f32[32,7168]{1,0:T(8,128)S(1)} %collective-permute-done.4.refs_0_, f32[32,7168]{1,0:T(8,128)S(1)} %collective-permute-done.5.refs_1_, f32[2,7168]{1,0:T(2,128)S(1)} %pad_maximum_fusion.refs_2_, f32[7168,384]{1,0:T(8,128)S(1)} %copy-done.1), custom_call_target="tpu_custom_call" | custom-call | tf_op jit(solution)/shard_map/pallas_call | solution.py:74
  55.8 3.9 %collective-permute-done.7.refs_1_ = f32[32,5376]{1,0:T(8,128)S(1)} collective-permute-done((f32[32,5376]{1,0:T(8,128)S(1)}, f32[32,5376]{1,0:T(8,128)S(1)}, u32[]{:S(2)}, u32[]{:S(2)}) %collective-permute-start.7) | collective-permute-done | bytes 688160 | tf_op jit(solution)/shard_map/ppermute | solution.py:165
  59.7 3.7 %collective-permute-done.6.refs_0_ = f32[32,5376]{1,0:T(8,128)S(1)} collective-permute-done((f32[32,5376]{1,0:T(8,128)S(1)}, f32[32,5376]{1,0:T(8,128)S(1)}, u32[]{:S(2)}, u32[]{:S(2)}) %collective-permute-start.6) | collective-permute-done | bytes 688160 | tf_op jit(solution)/shard_map/ppermute | solution.py:161
  63.5 2.6 %shard_map.68.refs_7_ = f32[64,384]{1,0:T(8,128)S(1)} custom-call(f32[32,5376]{1,0:T(8,128)S(1)} %collective-permute-done.6.refs_0_, f32[32,5376]{1,0:T(8,128)S(1)} %collective-permute-done.7.refs_1_, f32[2,7168]{1,0:T(2,128)S(1)} %pad_maximum_fusion.refs_2_, f32[7168,384]{1,0:T(8,128)S(1)} %copy-done.1), custom_call_target="tpu_custom_call" | custom-call | tf_op jit(solution)/shard_map/pallas_call | solution.py:74
  66.1 0.0 copy-start.5
  66.1 0.0 copy-start.6
  66.1 0.8 collective-permute-done.1.refs_0_
  66.9 0.9 shard_map.69
  67.8 0.1 collective-permute-start.8
  67.9 1.4 %collective-permute-done.8 = f32[32,4,384]{2,1,0:T(4,128)S(1)} collective-permute-done((f32[32,4,384]{2,1,0:T(4,128)S(1)}, f32[32,4,384]{2,1,0:T(4,128)S(1)}, u32[]{:S(2)}, u32[]{:S(2)}) %collective-permute-start.8) | collective-permute-done | bytes 196640 | tf_op jit(solution)/shard_map/ppermute | solution.py:169
  69.4 0.7 add.3
  70.1 11.4 %all-to-all-start = ((f32[32,4,384]{2,1,0:T(4,128)}), f32[32,4,384]{2,1,0:T(4,128)S(1)}, u32[]{:S(2)}, u32[]{:S(2)}) async-start(f32[32,4,384]{2,1,0:T(4,128)} %add.3), calls=%async_computation | async-start | bytes 393216 | tf_op jit(solution)/shard_map/all_to_all | solution.py:192
  81.5 11.3 %all-to-all-done.shares_ref = f32[32,4,384]{2,1,0:T(4,128)S(1)} async-done(((f32[32,4,384]{2,1,0:T(4,128)}), f32[32,4,384]{2,1,0:T(4,128)S(1)}, u32[]{:S(2)}, u32[]{:S(2)}) %all-to-all-start) | async-done | bytes 196640 | tf_op jit(solution)/shard_map/all_to_all | solution.py:192
  92.7 0.6 shard_map.70
  (20 shorter events, 0.2 us)
Async XLA Ops:
  0.0 4.7 %copy-start.2 = (f32[2,32,7168]{2,1,0:T(8,128)S(1)}, f32[2,32,7168]{2,1,0:T(8,128)}, u32[]{:S(2)}) copy-start(f32[2,32,7168]{2,1,0:T(8,128)} %own_ref.1) | copy-start | bytes 5505028
  0.0 4.6 %copy-start.4 = (s32[7168]{0:T(1024)S(1)}, s32[7168]{0:T(1024)}, u32[]{:S(2)}) copy-start(s32[7168]{0:T(1024)} %param.9) | copy-start | bytes 86020
  0.0 4.6 %copy-start.3 = (s32[7168]{0:T(1024)S(1)}, s32[7168]{0:T(1024)}, u32[]{:S(2)}) copy-start(s32[7168]{0:T(1024)} %param.8) | copy-start | bytes 86020
  1.7 23.6 %collective-permute-start.2 = (f32[32,7168]{1,0:T(8,128)S(1)}, f32[32,7168]{1,0:T(8,128)S(1)}, u32[]{:S(2)}, u32[]{:S(2)}) collective-permute-start(f32[32,7168]{1,0:T(8,128)S(1)} %get-tuple-element.15), channel_id=1, source_target_pairs={{0,3},{1,0},{2,1},{3,2},{4,7},{5,4},{6,5},{7,6},{8,11},{9,8},{10,9... | collective-permute-start | bytes 2752520 | tf_op jit(solution)/shard_map/ppermute | solution.py:165
  4.6 24.6 %collective-permute-start = (f32[32,7168]{1,0:T(8,128)S(1)}, f32[32,7168]{1,0:T(8,128)S(1)}, u32[]{:S(2)}, u32[]{:S(2)}) collective-permute-start(f32[32,7168]{1,0:T(8,128)S(1)} %get-tuple-element.16), channel_id=1, source_target_pairs={{0,1},{1,2},{2,3},{3,0},{4,5},{5,6},{6,7},{7,4},{8,9},{9,10},{10,1... | collective-permute-start | bytes 2752520 | tf_op jit(solution)/shard_map/ppermute | solution.py:161
  4.7 4.1 %copy-start = (f32[7168,384]{1,0:T(8,128)S(1)}, f32[7168,384]{1,0:T(8,128)}, u32[]{:S(2)}) copy-start(f32[7168,384]{1,0:T(8,128)} %refs_3_.9) | copy-start | bytes 33030148
  8.8 39.9 %copy-start.1 = (f32[7168,384]{1,0:T(8,128)S(1)}, f32[7168,384]{1,0:T(8,128)}, u32[]{:S(2)}) copy-start(f32[7168,384]{1,0:T(8,128)} %refs_3_.9) | copy-start | bytes 33030148
  12.8 35.9 %collective-permute-start.4 = (f32[32,7168]{1,0:T(8,128)S(1)}, f32[32,7168]{1,0:T(8,128)S(1)}, u32[]{:S(2)}, u32[]{:S(2)}) collective-permute-start(f32[32,7168]{1,0:T(8,128)S(1)} %get-tuple-element.9), channel_id=1, source_target_pairs={{0,1},{1,2},{2,3},{3,0},{4,5},{5,6},{6,7},{7,4},{8,9},{9,10},{10,1... | collective-permute-start | bytes 2752520 | tf_op jit(solution)/shard_map/ppermute | solution.py:161
  13.6 38.6 %collective-permute-start.5 = (f32[32,7168]{1,0:T(8,128)S(1)}, f32[32,7168]{1,0:T(8,128)S(1)}, u32[]{:S(2)}, u32[]{:S(2)}) collective-permute-start(f32[32,7168]{1,0:T(8,128)S(1)} %get-tuple-element.10), channel_id=1, source_target_pairs={{0,3},{1,0},{2,1},{3,2},{4,7},{5,4},{6,5},{7,6},{8,11},{9,8},{10,9... | collective-permute-start | bytes 2752520 | tf_op jit(solution)/shard_map/ppermute | solution.py:165
  25.4 34.4 %collective-permute-start.7 = (f32[32,5376]{1,0:T(8,128)S(1)}, f32[32,5376]{1,0:T(8,128)S(1)}, u32[]{:S(2)}, u32[]{:S(2)}) collective-permute-start(f32[32,5376]{1,0:T(8,128)S(1)} %slice.27), channel_id=1, source_target_pairs={{0,3},{1,0},{2,1},{3,2},{4,7},{5,4},{6,5},{7,6},{8,11},{9,8},{10,9... | collective-permute-start | bytes 2064392 | tf_op jit(solution)/shard_map/ppermute | solution.py:165
  29.2 34.3 %collective-permute-start.6 = (f32[32,5376]{1,0:T(8,128)S(1)}, f32[32,5376]{1,0:T(8,128)S(1)}, u32[]{:S(2)}, u32[]{:S(2)}) collective-permute-start(f32[32,5376]{1,0:T(8,128)S(1)} %slice.26), channel_id=1, source_target_pairs={{0,1},{1,2},{2,3},{3,0},{4,5},{5,6},{6,7},{7,4},{8,9},{9,10},{10,1... | collective-permute-start | bytes 2064392 | tf_op jit(solution)/shard_map/ppermute | solution.py:161
  29.3 36.8 %collective-permute-start.3 = (f32[32,1792]{1,0:T(8,128)S(1)}, f32[32,1792]{1,0:T(8,128)S(1)}, u32[]{:S(2)}, u32[]{:S(2)}) collective-permute-start(f32[32,1792]{1,0:T(8,128)S(1)} %slice.25), channel_id=1, source_target_pairs={{0,3},{1,0},{2,1},{3,2},{4,7},{5,4},{6,5},{7,6},{8,11},{9,8},{10,9... | collective-permute-start | bytes 688136 | tf_op jit(solution)/shard_map/ppermute | solution.py:165
  48.7 18.2 %collective-permute-start.1 = (f32[32,1792]{1,0:T(8,128)S(1)}, f32[32,1792]{1,0:T(8,128)S(1)}, u32[]{:S(2)}, u32[]{:S(2)}) collective-permute-start(f32[32,1792]{1,0:T(8,128)S(1)} %slice.24), channel_id=1, source_target_pairs={{0,1},{1,2},{2,3},{3,0},{4,5},{5,6},{6,7},{7,4},{8,9},{9,10},{10,1... | collective-permute-start | bytes 688136 | tf_op jit(solution)/shard_map/ppermute | solution.py:161
  66.1 15.3 %copy-start.5 = (s32[384]{0:T(512)S(1)}, s32[384]{0:T(512)}, u32[]{:S(2)}) copy-start(s32[384]{0:T(512)} %param.10) | copy-start | bytes 4612
  66.1 15.4 %copy-start.6 = (s32[384]{0:T(512)S(1)}, s32[384]{0:T(512)}, u32[]{:S(2)}) copy-start(s32[384]{0:T(512)} %param.11) | copy-start | bytes 4612
  67.8 1.5 %collective-permute-start.8 = (f32[32,4,384]{2,1,0:T(4,128)S(1)}, f32[32,4,384]{2,1,0:T(4,128)S(1)}, u32[]{:S(2)}, u32[]{:S(2)}) collective-permute-start(f32[32,4,384]{2,1,0:T(4,128)S(1)} %get-tuple-element.12), channel_id=1, source_target_pairs={{0,4},{4,0},{8,12},{12,8},{16,20},{20,16},{24,28},{28,24},{32,36},... | collective-permute-start | bytes 589832 | tf_op jit(solution)/shard_map/ppermute | solution.py:169
  70.1 22.7 %all-to-all-start = ((f32[32,4,384]{2,1,0:T(4,128)}), f32[32,4,384]{2,1,0:T(4,128)S(1)}, u32[]{:S(2)}, u32[]{:S(2)}) async-start(f32[32,4,384]{2,1,0:T(4,128)} %add.3), calls=%async_computation | async-start | bytes 393216 | tf_op jit(solution)/shard_map/all_to_all | solution.py:192

commit v3 on v2

v3 whole, which is shorter than its diff:
```python
import functools

import jax
import jax.numpy as jnp
from jax import lax
from jax.experimental import pallas as pl
from jax.experimental.pallas import tpu as pltpu
from jax.sharding import PartitionSpec as P

F32 = jnp.float32
BF16 = jnp.bfloat16
STEP = 1792
VMEM = pltpu.CompilerParams(vmem_limit_bytes=24 * 2**20)
FREE = pl.CostEstimate(flops=0, bytes_accessed=0, transcendentals=0)
GROUPS, LAYERS, CORES = 4, 8, 2


def halves(x):
    high = x.astype(BF16)
    return high, (x - high.astype(F32)).astype(BF16)


def products(rows, block):
    count = rows.shape[0]
    high, low = halves(rows)
    block_high, block_low = halves(block)
    first = jnp.dot(jnp.concatenate([high, low], axis=0), block_high, preferred_element_type=F32)
    return first[:count] + (first[count:] + jnp.dot(high, block_low, preferred_element_type=F32))


def add_step(slabs, piece_refs, weight_ref, block_ref, total_ref):
    rows = [
        ref[...].reshape(-1, ref.shape[-1]) * weight_ref[slab : slab + 1, :] for ref, slab in zip(piece_refs, slabs)
    ]
    total_ref[...] += products(jnp.concatenate(rows, axis=0), block_ref[...])


def sum_kernel(slabs, *refs):
    n, total_ref = len(slabs), refs[-1]

    @pl.when(pl.program_id(0) == 0)
    def _():
        total_ref[...] = jnp.zeros_like(total_ref)

    add_step(slabs, refs[:n], refs[n], refs[n + 1], total_ref)


def specs(piece_specs, columns, first):
    return piece_specs + [
        pl.BlockSpec((2, STEP), lambda k: (0, k + first)),
        pl.BlockSpec((STEP, columns), lambda k: (k + first, 0)),
    ]


def own_sums(amplitudes, weights, integrals, after):
    slabs, rows, pairs = amplitudes.shape
    columns = integrals.shape[1]
    own = [pl.BlockSpec((1, rows, STEP), lambda k, s=s: (s, 0, k)) for s in range(slabs)]
    return pl.pallas_call(
        functools.partial(sum_kernel, (0, 1)),
        grid=(pairs // STEP,),
        in_specs=specs(own, columns, 0) + [pl.BlockSpec(memory_space=pl.ANY)] * len(after),
        out_specs=pl.BlockSpec((slabs * rows, columns), lambda k: (0, 0)),
        out_shape=jax.ShapeDtypeStruct((slabs * rows, columns), F32),
        compiler_params=VMEM,
        cost_estimate=FREE,
    )(amplitudes, amplitudes, weights, integrals, *after)


def partial_sums(pieces, slabs, weights, integrals, first=0, after=()):
    n, (rows, pairs) = len(pieces), pieces[0].shape
    columns = integrals.shape[1]
    return pl.pallas_call(
        functools.partial(sum_kernel, slabs),
        grid=(pairs // STEP,),
        in_specs=specs([pl.BlockSpec((rows, STEP), lambda k: (0, k))] * n, columns, first)
        + [pl.BlockSpec(memory_space=pl.ANY)] * len(after),
        out_specs=pl.BlockSpec((n * rows, columns), lambda k: (0, 0)),
        out_shape=jax.ShapeDtypeStruct((n * rows, columns), F32),
        compiler_params=VMEM,
        cost_estimate=FREE,
    )(*pieces, weights, integrals, *after)


def lay_out(ref, start, slab, group, core, mine_ref, other_ref):
    for layer in range(LAYERS):
        pair = start + 2 * CORES * layer
        first, second = ref[pair : pair + 2, :], ref[pair + 2 : pair + 4, :]
        at = LAYERS * group + layer, slice(2 * slab, 2 * slab + 2)
        mine_ref[at] = jnp.where(core == 0, first, second)
        other_ref[at] = jnp.where(core == 0, second, first)


def exchange_kernel(own_ref, near_ref, far_ref, mine_ref, other_ref):
    me, core = lax.axis_index("ab"), lax.rem(lax.axis_index("cd"), CORES)
    opposite = pl.ds(LAYERS * lax.rem(me + 2, GROUPS), LAYERS)
    mine_ref[opposite] = jnp.zeros((LAYERS, *mine_ref.shape[1:]), F32)
    other_ref[opposite] = jnp.zeros((LAYERS, *mine_ref.shape[1:]), F32)
    for ref, start, away, slab in (
        (own_ref, 0, 0, 0),
        (own_ref, 32, 0, 1),
        (near_ref, 0, 3, 0),
        (near_ref, 32, 1, 1),
        (far_ref, 0, 3, 1),
        (far_ref, 32, 1, 0),
    ):
        lay_out(ref, start, slab, lax.rem(me + away, GROUPS), core, mine_ref, other_ref)


def exchange(own, near, far):
    shape = (GROUPS * LAYERS, 4, own.shape[1])
    return pl.pallas_call(
        exchange_kernel,
        out_shape=[jax.ShapeDtypeStruct(shape, F32)] * 2,
        compiler_params=VMEM,
        cost_estimate=FREE,
    )(own, near, far)


def opposite_kernel(slabs, *refs):
    n = len(slabs)
    before_ref, mine_ref, other_ref, total_ref = refs[n + 2 :]
    step = pl.program_id(0)

    @pl.when(step == 0)
    def _():
        total_ref[...] = before_ref[...]

    add_step(slabs, refs[:n], refs[n], refs[n + 1], total_ref)

    @pl.when(step == pl.num_programs(0) - 1)
    def _():
        core = lax.rem(lax.axis_index("cd"), CORES)
        for slab in range(2):
            lay_out(total_ref, 32 * slab, slab, 0, core, mine_ref, other_ref)


def opposite_sums(pieces, slabs, weights, integrals, first, before):
    n, (rows, pairs) = len(pieces), pieces[0].shape
    columns = integrals.shape[1]
    return pl.pallas_call(
        functools.partial(opposite_kernel, slabs),
        grid=(pairs // STEP,),
        in_specs=specs([pl.BlockSpec((rows, STEP), lambda k: (0, k))] * n, columns, first)
        + [pl.BlockSpec(before.shape, lambda k: (0, 0))],
        out_specs=[pl.BlockSpec((LAYERS, 4, columns), lambda k: (0, 0, 0))] * 2,
        out_shape=[jax.ShapeDtypeStruct((LAYERS, 4, columns), F32)] * 2,
        scratch_shapes=[pltpu.VMEM((n * rows, columns), F32)],
        compiler_params=VMEM,
        cost_estimate=FREE,
    )(*pieces, weights, integrals, before)


def last_kernel(mine_ref, got_ref, mine_opposite_ref, got_opposite_ref, out_ref):
    group = lax.rem(lax.axis_index("ab") + 2, GROUPS)
    out_ref[...] = mine_ref[...] + got_ref[...]
    out_ref[pl.ds(LAYERS * group, LAYERS)] = mine_opposite_ref[...] + got_opposite_ref[...]


def last_sums(*arrays):
    return pl.pallas_call(
        last_kernel,
        out_shape=jax.ShapeDtypeStruct(arrays[0].shape, F32),
        compiler_params=VMEM,
        cost_estimate=FREE,
    )(*arrays)


def finish_kernel(shares_ref, a_ref, b_ref, out_ref):
    keep = jnp.where(a_ref[...] == b_ref[...], F32(0.0), F32(0.5))
    summed = jnp.sum(shares_ref[...], axis=0)
    out_ref[:, 0, :] = 0.5 * summed[0:2]
    out_ref[:, 1, :] = keep * summed[2:4]


def pieces_kernel(own_ref, *refs):
    plus_ref, minus_ref = refs[-2:]
    plus_ref[...] = own_ref[0]
    minus_ref[...] = own_ref[1]


def slabs_after(amplitudes, pairs, *after):
    rows = amplitudes.shape[1]
    return pl.pallas_call(
        pieces_kernel,
        grid=(pairs // STEP,),
        in_specs=[pl.BlockSpec((2, rows, STEP), lambda k: (0, 0, k))] + [pl.BlockSpec(memory_space=pl.ANY)] * len(after),
        out_specs=[pl.BlockSpec((rows, STEP), lambda k: (0, k))] * 2,
        out_shape=[jax.ShapeDtypeStruct((rows, pairs), F32)] * 2,
        compiler_params=VMEM,
        cost_estimate=FREE,
    )(amplitudes, *after)


def right(x):
    return lax.ppermute(x, "ab", [(i, (i + 1) % GROUPS) for i in range(GROUPS)])


def left(x):
    return lax.ppermute(x, "ab", [(i, (i - 1) % GROUPS) for i in range(GROUPS)])


def over_cores(x):
    return lax.ppermute(x, "cd", [(i, i ^ 1) for i in range(GROUPS * LAYERS * CORES)])


def local(amplitudes, integrals, c_index, d_index, a_index, b_index):
    pairs, columns = integrals.shape
    cut = pairs - STEP

    same = c_index == d_index
    weights = jnp.stack([jnp.where(same, F32(0.5), F32(1.0)), jnp.where(same, F32(0.0), F32(1.0))])

    right_last, left_last = right(amplitudes[0, :, cut:]), left(amplitudes[1, :, cut:])
    plus, minus = slabs_after(amplitudes, cut)
    right_plus, left_minus = right(plus), left(minus)
    own = own_sums(amplitudes, weights, integrals, (right_last, left_last))
    plus, minus = slabs_after(amplitudes, pairs, own)
    right_minus, left_plus = right(minus), left(plus)
    onward = [right(right_plus), left(left_minus)]
    onward_last = [right(right_last), left(left_last)]

    near = partial_sums([right_plus, left_minus], (0, 1), weights, integrals)
    near = partial_sums([right_last, left_last], (0, 1), weights, integrals, cut // STEP) + near
    far = partial_sums([right_minus, left_plus], (1, 0), weights, integrals)
    mine, other = exchange(own, near, far)
    got = over_cores(other)
    opposite = partial_sums(onward, (0, 1), weights, integrals, 0, (got,))
    mine_opposite, other = opposite_sums(onward_last, (0, 1), weights, integrals, cut // STEP, opposite)
    part_sum = last_sums(mine, got, mine_opposite, over_cores(other))

    planes = [[2 * i + core for i in range(GROUPS * LAYERS)] for core in range(CORES)]
    shares = lax.all_to_all(part_sum, "cd", 0, 0, tiled=True, axis_index_groups=planes)
    return pl.pallas_call(
        finish_kernel, out_shape=jax.ShapeDtypeStruct((2, 2, columns), F32), compiler_params=VMEM, cost_estimate=FREE
    )(shares, a_index.reshape(1, columns), b_index.reshape(1, columns))


def solution(mesh):
    placed = (P(None, "ab", "cd"), P("cd", "ab"), P("cd"), P("cd"), P("ab"), P("ab"))
    return jax.shard_map(local, mesh=mesh, in_specs=placed, out_specs=P("cd", None, "ab"), check_vma=False)
```

time: 93.6 us -> 91 us (0.972)
  waiting for transfers between devices: 46.3 us -> 40.2 us
  starting transfers between devices: 24.8 us -> 26.5 us
  Pallas kernels: 15.2 us -> 16.3 us
    ppermute x4 -> x5, waiting for transfers between devices: 13.1 us -> 8.94 us  [left(): return lax.ppermute(x, 'ab', [(i, (i - 1) % GROUPS) for i in range(GROUPS)])]
    ppermute x4 -> x5, waiting for transfers between devices: 20.6 us -> 17.3 us  [right(): return lax.ppermute(x, 'ab', [(i, (i + 1) % GROUPS) for i in range(GROUPS)])]
    ppermute x4 -> x5, starting transfers between devices: 0.91 us -> 3.91 us  [right(): return lax.ppermute(x, 'ab', [(i, (i + 1) % GROUPS) for i in range(GROUPS)])]
    ppermute x4 -> x5, starting transfers between devices: 12.5 us -> 10.9 us  [left(): return lax.ppermute(x, 'ab', [(i, (i - 1) % GROUPS) for i in range(GROUPS)])]
    unnamed x14, local copies, waits for them, and re-layouts: 4.15 us -> 5.65 us
    ppermute x1 -> x2, waiting for transfers between devices: 1.43 us -> 2.65 us  [over_cores(): lax.ppermute(x, 'cd', [(i, i ^ 1) for i in range(GROUPS * LAYERS * CORES)])]
    pallas_call x3 -> x4, Pallas kernels: 9.67 us -> 9.63 us  [partial_sums(): pl.pallas_call(functools.partial(sum_kernel, slabs), grid=(pairs // STEP,...]
  transfers between devices with their start and end apart: 10 -> 13, of which waited for: 7 -> 10; matrix products, arithmetic and copies ran while one was open for 0% -> 0% of each run, Pallas kernels for 15% -> 16%
where the time goes in v3:
time: 91 us; the launch traced here: 90 us
  waiting for transfers between devices  40.2 us (44%)
  starting transfers between devices  26.5 us (29%)
  Pallas kernels  16.3 us (18%)
  local copies, waits for them, and re-layouts  6.74 us (7%)
    ppermute x5, waiting for transfers between devices, right(): return lax.ppermute(x, 'ab', [(i, (i + 1) % GROUPS) for i in range(GROUPS)])  17.3 us
    all_to_all x1, starting transfers between devices, local(): lax.all_to_all(part_sum, 'cd', 0, 0, tiled=True, axis_index_groups=planes)  11.4 us
    all_to_all x1, waiting for transfers between devices, local(): lax.all_to_all(part_sum, 'cd', 0, 0, tiled=True, axis_index_groups=planes)  11.3 us
    ppermute x5, starting transfers between devices, left(): return lax.ppermute(x, 'ab', [(i, (i - 1) % GROUPS) for i in range(GROUPS)])  10.9 us
    pallas_call x4, Pallas kernels, partial_sums(): pl.pallas_call(functools.partial(sum_kernel, slabs), grid=(pairs // STEP,...  9.63 us
    ppermute x5, waiting for transfers between devices, left(): return lax.ppermute(x, 'ab', [(i, (i - 1) % GROUPS) for i in range(GROUPS)])  8.94 us
    unnamed x14, local copies, waits for them, and re-layouts  5.65 us
    ppermute x5, starting transfers between devices, right(): return lax.ppermute(x, 'ab', [(i, (i + 1) % GROUPS) for i in range(GROUPS)])  3.91 us
  transfers between devices with their start and end apart: 13, of which 10 were waited for; matrix products, arithmetic and copies ran while one was open for 0% of the time, Pallas kernels for 16%

profile of v3, /device:TPU:32, one launch (start us, length us, event | category | flops | bytes accessed | tf_op | source)
XLA Modules:
  0.0 90.0 jit_solution(10986977435149171528)
XLA Ops:
  0.0 1.1 %slice_bitcast_fusion = (f32[32,1792]{1,0:T(8,128)S(1)}, f32[32,1792]{1,0:T(8,128)S(1)}) fusion(f32[2,32,7168]{2,1,0:T(8,128)} %own_ref.3), kind=kLoop, calls=%fused_computation | loop fusion | bytes 917504 | tf_op jit(solution)/shard_map/squeeze | solution.py:214
  1.1 1.6 %collective-permute-start = (f32[32,1792]{1,0:T(8,128)S(1)}, f32[32,1792]{1,0:T(8,128)S(1)}, u32[]{:S(2)}, u32[]{:S(2)}) collective-permute-start(f32[32,1792]{1,0:T(8,128)S(1)} %get-tuple-element.24), channel_id=1, source_target_pairs={{0,1},{1,2},{2,3},{3,0},{4,5},{5,6},{6,7},{7,4},{8,9},{9,10},{10,1... | collective-permute-start | bytes 688136 | tf_op jit(solution)/shard_map/ppermute | solution.py:196
  2.7 1.7 %collective-permute-start.1 = (f32[32,1792]{1,0:T(8,128)S(1)}, f32[32,1792]{1,0:T(8,128)S(1)}, u32[]{:S(2)}, u32[]{:S(2)}) collective-permute-start(f32[32,1792]{1,0:T(8,128)S(1)} %get-tuple-element.23), channel_id=1, source_target_pairs={{0,3},{1,0},{2,1},{3,2},{4,7},{5,4},{6,5},{7,6},{8,11},{9,8},{10,9... | collective-permute-start | bytes 688136 | tf_op jit(solution)/shard_map/ppermute | solution.py:200
  4.4 1.5 %copy-done.2 = f32[2,32,7168]{2,1,0:T(8,128)S(1)} copy-done((f32[2,32,7168]{2,1,0:T(8,128)S(1)}, f32[2,32,7168]{2,1,0:T(8,128)}, u32[]{:S(2)}) %copy-start.2) | copy-done | bytes 1835032
  5.9 0.4 shard_map.66
  6.3 0.4 collective-permute-start.2
  6.6 3.0 %collective-permute-start.3 = (f32[32,5376]{1,0:T(8,128)S(1)}, f32[32,5376]{1,0:T(8,128)S(1)}, u32[]{:S(2)}, u32[]{:S(2)}) collective-permute-start(f32[32,5376]{1,0:T(8,128)S(1)} %get-tuple-element.14), channel_id=1, source_target_pairs={{0,3},{1,0},{2,1},{3,2},{4,7},{5,4},{6,5},{7,6},{8,11},{9,8},{10,9... | collective-permute-start | bytes 2064392 | tf_op jit(solution)/shard_map/ppermute | solution.py:200
  9.7 0.3 collective-permute-done.refs_4_.refs_0_
  10.0 1.1 %collective-permute-done.1.refs_5_.refs_1_ = f32[32,1792]{1,0:T(8,128)S(1)} collective-permute-done((f32[32,1792]{1,0:T(8,128)S(1)}, f32[32,1792]{1,0:T(8,128)S(1)}, u32[]{:S(2)}, u32[]{:S(2)}) %collective-permute-start.1) | collective-permute-done | bytes 229408 | tf_op jit(solution)/shard_map/ppermute | solution.py:200
  11.1 4.1 %copy-done = f32[7168,384]{1,0:T(8,128)S(1)} copy-done((f32[7168,384]{1,0:T(8,128)S(1)}, f32[7168,384]{1,0:T(8,128)}, u32[]{:S(2)}) %copy-start) | copy-done | bytes 11010072
  15.2 3.5 %shard_map.64.refs_0_.own_ref = f32[64,384]{1,0:T(8,128)S(1)} custom-call(f32[2,32,7168]{2,1,0:T(8,128)S(1)} %copy-done.2, f32[2,32,7168]{2,1,0:T(8,128)S(1)} %copy-done.2, f32[2,7168]{1,0:T(2,128)S(1)} %pad_maximum_fusion.refs_2_, f32[7168,384]{1,0:T(8,128)S(1)} %copy-done, f32[32,1792]{1,0:T(8,128)S(1)} %collective-permute-done.refs_4_.refs_0_, ...), custom_call_target="tpu_custom_call" | custom-call | tf_op jit(solution)/shard_map/pallas_call | solution.py:59
  18.7 0.5 shard_map.68
  19.2 1.7 %collective-permute-start.4 = (f32[32,7168]{1,0:T(8,128)S(1)}, f32[32,7168]{1,0:T(8,128)S(1)}, u32[]{:S(2)}, u32[]{:S(2)}) collective-permute-start(f32[32,7168]{1,0:T(8,128)S(1)} %get-tuple-element.15), channel_id=1, source_target_pairs={{0,1},{1,2},{2,3},{3,0},{4,5},{5,6},{6,7},{7,4},{8,9},{9,10},{10,1... | collective-permute-start | bytes 2752520 | tf_op jit(solution)/shard_map/ppermute | solution.py:196
  20.9 1.6 %collective-permute-start.5 = (f32[32,7168]{1,0:T(8,128)S(1)}, f32[32,7168]{1,0:T(8,128)S(1)}, u32[]{:S(2)}, u32[]{:S(2)}) collective-permute-start(f32[32,7168]{1,0:T(8,128)S(1)} %get-tuple-element.16), channel_id=1, source_target_pairs={{0,3},{1,0},{2,1},{3,2},{4,7},{5,4},{6,5},{7,6},{8,11},{9,8},{10,9... | collective-permute-start | bytes 2752520 | tf_op jit(solution)/shard_map/ppermute | solution.py:200
  22.5 3.3 %collective-permute-done.3.refs_1_ = f32[32,5376]{1,0:T(8,128)S(1)} collective-permute-done((f32[32,5376]{1,0:T(8,128)S(1)}, f32[32,5376]{1,0:T(8,128)S(1)}, u32[]{:S(2)}, u32[]{:S(2)}) %collective-permute-start.3) | collective-permute-done | bytes 688160 | tf_op jit(solution)/shard_map/ppermute | solution.py:200
  25.8 3.3 %collective-permute-start.10 = (f32[32,5376]{1,0:T(8,128)S(1)}, f32[32,5376]{1,0:T(8,128)S(1)}, u32[]{:S(2)}, u32[]{:S(2)}) collective-permute-start(f32[32,5376]{1,0:T(8,128)S(1)} %collective-permute-done.3.refs_1_), channel_id=1, source_target_pairs={{0,3},{1,0},{2,1},{3,2},{4,7},{5,4},{6,5},{7,6},{8,11},{9,8},{10,9... | collective-permute-start | bytes 2064392 | tf_op jit(solution)/shard_map/ppermute | solution.py:200
  29.2 0.3 collective-permute-start.7
  29.5 16.1 %collective-permute-done.4.refs_0_ = f32[32,7168]{1,0:T(8,128)S(1)} collective-permute-done((f32[32,7168]{1,0:T(8,128)S(1)}, f32[32,7168]{1,0:T(8,128)S(1)}, u32[]{:S(2)}, u32[]{:S(2)}) %collective-permute-start.4) | collective-permute-done | bytes 917536 | tf_op jit(solution)/shard_map/ppermute | solution.py:196
  45.6 1.2 %collective-permute-start.8 = (f32[32,1792]{1,0:T(8,128)S(1)}, f32[32,1792]{1,0:T(8,128)S(1)}, u32[]{:S(2)}, u32[]{:S(2)}) collective-permute-start(f32[32,1792]{1,0:T(8,128)S(1)} %collective-permute-done.1.refs_5_.refs_1_), channel_id=1, source_target_pairs={{0,3},{1,0},{2,1},{3,2},{4,7},{5,4},{6,5},{7,6},{8,11},{9,8},{10,9... | collective-permute-start | bytes 688136 | tf_op jit(solution)/shard_map/ppermute | solution.py:200
  46.8 0.8 shard_map.65
  47.7 2.7 %shard_map.67 = f32[64,384]{1,0:T(8,128)S(1)} custom-call(f32[32,5376]{1,0:T(8,128)S(1)} %collective-permute-done.2.refs_0_, f32[32,5376]{1,0:T(8,128)S(1)} %collective-permute-done.3.refs_1_, f32[2,7168]{1,0:T(2,128)S(1)} %pad_maximum_fusion.refs_2_, f32[7168,384]{1,0:T(8,128)S(1)} %copy-done.1), custom_call_target="tpu_custom_call" | custom-call | tf_op jit(solution)/shard_map/pallas_call | solution.py:73
  50.4 3.5 %shard_map.69.far_ref = f32[64,384]{1,0:T(8,128)S(1)} custom-call(f32[32,7168]{1,0:T(8,128)S(1)} %collective-permute-done.4.refs_0_, f32[32,7168]{1,0:T(8,128)S(1)} %collective-permute-done.5.refs_1_, f32[2,7168]{1,0:T(2,128)S(1)} %pad_maximum_fusion.refs_2_, f32[7168,384]{1,0:T(8,128)S(1)} %copy-done.1), custom_call_target="tpu_custom_call" | custom-call | tf_op jit(solution)/shard_map/pallas_call | solution.py:73
  54.3 1.4 %collective-permute-done.6.refs_4_.got_ref = f32[32,4,384]{2,1,0:T(4,128)S(1)} collective-permute-done((f32[32,4,384]{2,1,0:T(4,128)S(1)}, f32[32,4,384]{2,1,0:T(4,128)S(1)}, u32[]{:S(2)}, u32[]{:S(2)}) %collective-permute-start.6) | collective-permute-done | bytes 196640 | tf_op jit(solution)/shard_map/ppermute | solution.py:204
  55.7 4.5 %collective-permute-done.10.refs_1_ = f32[32,5376]{1,0:T(8,128)S(1)} collective-permute-done((f32[32,5376]{1,0:T(8,128)S(1)}, f32[32,5376]{1,0:T(8,128)S(1)}, u32[]{:S(2)}, u32[]{:S(2)}) %collective-permute-start.10) | collective-permute-done | bytes 688160 | tf_op jit(solution)/shard_map/ppermute | solution.py:200
  60.3 2.6 %shard_map.71.refs_4_ = f32[64,384]{1,0:T(8,128)S(1)} custom-call(f32[32,5376]{1,0:T(8,128)S(1)} %collective-permute-done.9.refs_0_, f32[32,5376]{1,0:T(8,128)S(1)} %collective-permute-done.10.refs_1_, f32[2,7168]{1,0:T(2,128)S(1)} %pad_maximum_fusion.refs_2_, f32[7168,384]{1,0:T(8,128)S(1)} %copy-done.1, ...), custom_call_target="tpu_custom_call" | custom-call | tf_op jit(solution)/shard_map/pallas_call | solution.py:73
  63.0 0.8 collective-permute-done.7.refs_0_
  63.8 0.9 shard_map.72
  64.8 1.2 %collective-permute-done.11.got_opposite_ref = f32[8,4,384]{2,1,0:T(4,128)S(1)} collective-permute-done((f32[8,4,384]{2,1,0:T(4,128)S(1)}, f32[8,4,384]{2,1,0:T(4,128)S(1)}, u32[]{:S(2)}, u32[]{:S(2)}) %collective-permute-start.11) | collective-permute-done | bytes 49184 | tf_op jit(solution)/shard_map/ppermute | solution.py:204
  66.0 0.7 shard_map.73
  66.7 11.4 %all-to-all-start = ((f32[32,4,384]{2,1,0:T(4,128)}), f32[32,4,384]{2,1,0:T(4,128)S(1)}, u32[]{:S(2)}, u32[]{:S(2)}) async-start(f32[32,4,384]{2,1,0:T(4,128)} %shard_map.73), calls=%async_computation | async-start | bytes 393216 | tf_op jit(solution)/shard_map/all_to_all | solution.py:233
  78.1 11.3 %all-to-all-done.shares_ref = f32[32,4,384]{2,1,0:T(4,128)S(1)} async-done(((f32[32,4,384]{2,1,0:T(4,128)}), f32[32,4,384]{2,1,0:T(4,128)S(1)}, u32[]{:S(2)}, u32[]{:S(2)}) %all-to-all-start) | async-done | bytes 196640 | tf_op jit(solution)/shard_map/all_to_all | solution.py:233
  89.4 0.6 shard_map.74
  (26 shorter events, 0.7 us)
Async XLA Ops:
  0.0 9.6 %copy-start.3 = (s32[7168]{0:T(1024)S(1)}, s32[7168]{0:T(1024)}, u32[]{:S(2)}) copy-start(s32[7168]{0:T(1024)} %param.8) | copy-start | bytes 86020
  0.0 9.6 %copy-start.4 = (s32[7168]{0:T(1024)S(1)}, s32[7168]{0:T(1024)}, u32[]{:S(2)}) copy-start(s32[7168]{0:T(1024)} %param.9) | copy-start | bytes 86020
  1.1 8.9 %collective-permute-start = (f32[32,1792]{1,0:T(8,128)S(1)}, f32[32,1792]{1,0:T(8,128)S(1)}, u32[]{:S(2)}, u32[]{:S(2)}) collective-permute-start(f32[32,1792]{1,0:T(8,128)S(1)} %get-tuple-element.24), channel_id=1, source_target_pairs={{0,1},{1,2},{2,3},{3,0},{4,5},{5,6},{6,7},{7,4},{8,9},{9,10},{10,1... | collective-permute-start | bytes 688136 | tf_op jit(solution)/shard_map/ppermute | solution.py:196
  2.7 8.4 %collective-permute-start.1 = (f32[32,1792]{1,0:T(8,128)S(1)}, f32[32,1792]{1,0:T(8,128)S(1)}, u32[]{:S(2)}, u32[]{:S(2)}) collective-permute-start(f32[32,1792]{1,0:T(8,128)S(1)} %get-tuple-element.23), channel_id=1, source_target_pairs={{0,3},{1,0},{2,1},{3,2},{4,7},{5,4},{6,5},{7,6},{8,11},{9,8},{10,9... | collective-permute-start | bytes 688136 | tf_op jit(solution)/shard_map/ppermute | solution.py:200
  4.4 1.5 %copy-start.2 = (f32[2,32,7168]{2,1,0:T(8,128)S(1)}, f32[2,32,7168]{2,1,0:T(8,128)}, u32[]{:S(2)}) copy-start(f32[2,32,7168]{2,1,0:T(8,128)} %own_ref.3) | copy-start | bytes 5505028
  6.3 22.9 %collective-permute-start.2 = (f32[32,5376]{1,0:T(8,128)S(1)}, f32[32,5376]{1,0:T(8,128)S(1)}, u32[]{:S(2)}, u32[]{:S(2)}) collective-permute-start(f32[32,5376]{1,0:T(8,128)S(1)} %get-tuple-element.13), channel_id=1, source_target_pairs={{0,1},{1,2},{2,3},{3,0},{4,5},{5,6},{6,7},{7,4},{8,9},{9,10},{10,1... | collective-permute-start | bytes 2064392 | tf_op jit(solution)/shard_map/ppermute | solution.py:196
  6.6 19.2 %collective-permute-start.3 = (f32[32,5376]{1,0:T(8,128)S(1)}, f32[32,5376]{1,0:T(8,128)S(1)}, u32[]{:S(2)}, u32[]{:S(2)}) collective-permute-start(f32[32,5376]{1,0:T(8,128)S(1)} %get-tuple-element.14), channel_id=1, source_target_pairs={{0,3},{1,0},{2,1},{3,2},{4,7},{5,4},{6,5},{7,6},{8,11},{9,8},{10,9... | collective-permute-start | bytes 2064392 | tf_op jit(solution)/shard_map/ppermute | solution.py:200
  11.1 4.1 %copy-start = (f32[7168,384]{1,0:T(8,128)S(1)}, f32[7168,384]{1,0:T(8,128)}, u32[]{:S(2)}) copy-start(f32[7168,384]{1,0:T(8,128)} %refs_3_.11) | copy-start | bytes 33030148
  15.2 31.6 %copy-start.1 = (f32[7168,384]{1,0:T(8,128)S(1)}, f32[7168,384]{1,0:T(8,128)}, u32[]{:S(2)}) copy-start(f32[7168,384]{1,0:T(8,128)} %refs_3_.11) | copy-start | bytes 33030148
  19.2 26.4 %collective-permute-start.4 = (f32[32,7168]{1,0:T(8,128)S(1)}, f32[32,7168]{1,0:T(8,128)S(1)}, u32[]{:S(2)}, u32[]{:S(2)}) collective-permute-start(f32[32,7168]{1,0:T(8,128)S(1)} %get-tuple-element.15), channel_id=1, source_target_pairs={{0,1},{1,2},{2,3},{3,0},{4,5},{5,6},{6,7},{7,4},{8,9},{9,10},{10,1... | collective-permute-start | bytes 2752520 | tf_op jit(solution)/shard_map/ppermute | solution.py:196
  20.9 29.4 %collective-permute-start.5 = (f32[32,7168]{1,0:T(8,128)S(1)}, f32[32,7168]{1,0:T(8,128)S(1)}, u32[]{:S(2)}, u32[]{:S(2)}) collective-permute-start(f32[32,7168]{1,0:T(8,128)S(1)} %get-tuple-element.16), channel_id=1, source_target_pairs={{0,3},{1,0},{2,1},{3,2},{4,7},{5,4},{6,5},{7,6},{8,11},{9,8},{10,9... | collective-permute-start | bytes 2752520 | tf_op jit(solution)/shard_map/ppermute | solution.py:200
  25.8 34.4 %collective-permute-start.10 = (f32[32,5376]{1,0:T(8,128)S(1)}, f32[32,5376]{1,0:T(8,128)S(1)}, u32[]{:S(2)}, u32[]{:S(2)}) collective-permute-start(f32[32,5376]{1,0:T(8,128)S(1)} %collective-permute-done.3.refs_1_), channel_id=1, source_target_pairs={{0,3},{1,0},{2,1},{3,2},{4,7},{5,4},{6,5},{7,6},{8,11},{9,8},{10,9... | collective-permute-start | bytes 2064392 | tf_op jit(solution)/shard_map/ppermute | solution.py:200
  29.2 31.2 %collective-permute-start.9 = (f32[32,5376]{1,0:T(8,128)S(1)}, f32[32,5376]{1,0:T(8,128)S(1)}, u32[]{:S(2)}, u32[]{:S(2)}) collective-permute-start(f32[32,5376]{1,0:T(8,128)S(1)} %collective-permute-done.2.refs_0_), channel_id=1, source_target_pairs={{0,1},{1,2},{2,3},{3,0},{4,5},{5,6},{6,7},{7,4},{8,9},{9,10},{10,1... | collective-permute-start | bytes 2064392 | tf_op jit(solution)/shard_map/ppermute | solution.py:196
  29.2 34.6 %collective-permute-start.7 = (f32[32,1792]{1,0:T(8,128)S(1)}, f32[32,1792]{1,0:T(8,128)S(1)}, u32[]{:S(2)}, u32[]{:S(2)}) collective-permute-start(f32[32,1792]{1,0:T(8,128)S(1)} %collective-permute-done.refs_4_.refs_0_), channel_id=1, source_target_pairs={{0,1},{1,2},{2,3},{3,0},{4,5},{5,6},{6,7},{7,4},{8,9},{9,10},{10,1... | collective-permute-start | bytes 688136 | tf_op jit(solution)/shard_map/ppermute | solution.py:196
  45.6 18.2 %collective-permute-start.8 = (f32[32,1792]{1,0:T(8,128)S(1)}, f32[32,1792]{1,0:T(8,128)S(1)}, u32[]{:S(2)}, u32[]{:S(2)}) collective-permute-start(f32[32,1792]{1,0:T(8,128)S(1)} %collective-permute-done.1.refs_5_.refs_1_), channel_id=1, source_target_pairs={{0,3},{1,0},{2,1},{3,2},{4,7},{5,4},{6,5},{7,6},{8,11},{9,8},{10,9... | collective-permute-start | bytes 688136 | tf_op jit(solution)/shard_map/ppermute | solution.py:200
  54.0 1.7 %collective-permute-start.6 = (f32[32,4,384]{2,1,0:T(4,128)S(1)}, f32[32,4,384]{2,1,0:T(4,128)S(1)}, u32[]{:S(2)}, u32[]{:S(2)}) collective-permute-start(f32[32,4,384]{2,1,0:T(4,128)S(1)} %get-tuple-element.18), channel_id=1, source_target_pairs={{0,4},{4,0},{8,12},{12,8},{16,20},{20,16},{24,28},{28,24},{32,36},... | collective-permute-start | bytes 589832 | tf_op jit(solution)/shard_map/ppermute | solution.py:204
  63.0 15.1 %copy-start.5 = (s32[384]{0:T(512)S(1)}, s32[384]{0:T(512)}, u32[]{:S(2)}) copy-start(s32[384]{0:T(512)} %param.10) | copy-start | bytes 4612
  63.0 15.1 %copy-start.6 = (s32[384]{0:T(512)S(1)}, s32[384]{0:T(512)}, u32[]{:S(2)}) copy-start(s32[384]{0:T(512)} %param.11) | copy-start | bytes 4612
  64.7 1.3 %collective-permute-start.11 = (f32[8,4,384]{2,1,0:T(4,128)S(1)}, f32[8,4,384]{2,1,0:T(4,128)S(1)}, u32[]{:S(2)}, u32[]{:S(2)}) collective-permute-start(f32[8,4,384]{2,1,0:T(4,128)S(1)} %get-tuple-element.20), channel_id=1, source_target_pairs={{0,4},{4,0},{8,12},{12,8},{16,20},{20,16},{24,28},{28,24},{32,36},... | collective-permute-start | bytes 147464 | tf_op jit(solution)/shard_map/ppermute | solution.py:204
  66.7 22.7 %all-to-all-start = ((f32[32,4,384]{2,1,0:T(4,128)}), f32[32,4,384]{2,1,0:T(4,128)S(1)}, u32[]{:S(2)}, u32[]{:S(2)}) async-start(f32[32,4,384]{2,1,0:T(4,128)} %shard_map.73), calls=%async_computation | async-start | bytes 393216 | tf_op jit(solution)/shard_map/all_to_all | solution.py:233

commit v4 on v3

--- a/solution.py
+++ b/solution.py
@@ -13,6 +13,7 @@
 VMEM = pltpu.CompilerParams(vmem_limit_bytes=24 * 2**20)
 FREE = pl.CostEstimate(flops=0, bytes_accessed=0, transcendentals=0)
 GROUPS, LAYERS, CORES = 4, 8, 2
+ORDER = (4, 5, 6, 7, 0, 1, 2, 3)
 
 
 def halves(x):
@@ -82,20 +83,25 @@
     )(*pieces, weights, integrals, *after)
 
 
-def lay_out(ref, start, slab, group, core, mine_ref, other_ref):
+def place(layer, group):
+    return GROUPS * ORDER.index(layer) + GROUPS - 1 - group
+
+
+def lay_out(ref, start, slab, at, core, mine_ref, other_ref):
     for layer in range(LAYERS):
         pair = start + 2 * CORES * layer
         first, second = ref[pair : pair + 2, :], ref[pair + 2 : pair + 4, :]
-        at = LAYERS * group + layer, slice(2 * slab, 2 * slab + 2)
-        mine_ref[at] = jnp.where(core == 0, first, second)
-        other_ref[at] = jnp.where(core == 0, second, first)
+        half = slice(2 * slab, 2 * slab + 2)
+        mine_ref[at(layer), half] = jnp.where(core == 0, first, second)
+        other_ref[at(layer), half] = jnp.where(core == 0, second, first)
 
 
 def exchange_kernel(own_ref, near_ref, far_ref, mine_ref, other_ref):
     me, core = lax.axis_index("ab"), lax.rem(lax.axis_index("cd"), CORES)
-    opposite = pl.ds(LAYERS * lax.rem(me + 2, GROUPS), LAYERS)
-    mine_ref[opposite] = jnp.zeros((LAYERS, *mine_ref.shape[1:]), F32)
-    other_ref[opposite] = jnp.zeros((LAYERS, *mine_ref.shape[1:]), F32)
+    for layer in range(LAYERS):
+        opposite = place(layer, lax.rem(me + 2, GROUPS))
+        mine_ref[opposite] = jnp.zeros(mine_ref.shape[1:], F32)
+        other_ref[opposite] = jnp.zeros(mine_ref.shape[1:], F32)
     for ref, start, away, slab in (
         (own_ref, 0, 0, 0),
         (own_ref, 32, 0, 1),
@@ -104,7 +110,8 @@
         (far_ref, 0, 3, 1),
         (far_ref, 32, 1, 0),
     ):
-        lay_out(ref, start, slab, lax.rem(me + away, GROUPS), core, mine_ref, other_ref)
+        group = lax.rem(me + away, GROUPS)
+        lay_out(ref, start, slab, functools.partial(place, group=group), core, mine_ref, other_ref)
 
 
 def exchange(own, near, far):
@@ -132,7 +139,7 @@
     def _():
         core = lax.rem(lax.axis_index("cd"), CORES)
         for slab in range(2):
-            lay_out(total_ref, 32 * slab, slab, 0, core, mine_ref, other_ref)
+            lay_out(total_ref, 32 * slab, slab, lambda layer: layer, core, mine_ref, other_ref)
 
 
 def opposite_sums(pieces, slabs, weights, integrals, first, before):
@@ -154,7 +161,8 @@
 def last_kernel(mine_ref, got_ref, mine_opposite_ref, got_opposite_ref, out_ref):
     group = lax.rem(lax.axis_index("ab") + 2, GROUPS)
     out_ref[...] = mine_ref[...] + got_ref[...]
-    out_ref[pl.ds(LAYERS * group, LAYERS)] = mine_opposite_ref[...] + got_opposite_ref[...]
+    for layer in range(LAYERS):
+        out_ref[place(layer, group)] = mine_opposite_ref[layer] + got_opposite_ref[layer]
 
 
 def last_sums(*arrays):
@@ -229,7 +237,9 @@
     mine_opposite, other = opposite_sums(onward_last, (0, 1), weights, integrals, cut // STEP, opposite)
     part_sum = last_sums(mine, got, mine_opposite, over_cores(other))
 
-    planes = [[2 * i + core for i in range(GROUPS * LAYERS)] for core in range(CORES)]
+    planes = [
+        [CORES * (LAYERS * group + layer) + core for layer in ORDER for group in reversed(range(GROUPS))] for core in range(CORES)
+    ]
     shares = lax.all_to_all(part_sum, "cd", 0, 0, tiled=True, axis_index_groups=planes)
     return pl.pallas_call(
         finish_kernel, out_shape=jax.ShapeDtypeStruct((2, 2, columns), F32), compiler_params=VMEM, cost_estimate=FREE

time: 91 us -> 87.3 us (0.959)
  waiting for transfers between devices: 40.2 us -> 35.1 us
  starting transfers between devices: 26.5 us -> 27.5 us
    all_to_all x1, waiting for transfers between devices: 11.3 us -> 6.24 us  [local(): lax.all_to_all(part_sum, 'cd', 0, 0, tiled=True, axis_index_groups=planes)]
    all_to_all x1, starting transfers between devices: 11.4 us -> 12.4 us  [local(): lax.all_to_all(part_sum, 'cd', 0, 0, tiled=True, axis_index_groups=planes)]
where the time goes in v4:
time: 87.3 us; the launch traced here: 86 us
  waiting for transfers between devices  35.1 us (40%)
  starting transfers between devices  27.5 us (32%)
  Pallas kernels  16.3 us (19%)
  local copies, waits for them, and re-layouts  6.74 us (8%)
    ppermute x5, waiting for transfers between devices, right(): return lax.ppermute(x, 'ab', [(i, (i + 1) % GROUPS) for i in range(GROUPS)])  17.3 us
    all_to_all x1, starting transfers between devices, local(): lax.all_to_all(part_sum, 'cd', 0, 0, tiled=True, axis_index_groups=planes)  12.4 us
    ppermute x5, starting transfers between devices, left(): return lax.ppermute(x, 'ab', [(i, (i - 1) % GROUPS) for i in range(GROUPS)])  10.9 us
    pallas_call x4, Pallas kernels, partial_sums(): pl.pallas_call(functools.partial(sum_kernel, slabs), grid=(pairs // STEP,...  9.63 us
    ppermute x5, waiting for transfers between devices, left(): return lax.ppermute(x, 'ab', [(i, (i - 1) % GROUPS) for i in range(GROUPS)])  8.95 us
    all_to_all x1, waiting for transfers between devices, local(): lax.all_to_all(part_sum, 'cd', 0, 0, tiled=True, axis_index_groups=planes)  6.24 us
    unnamed x14, local copies, waits for them, and re-layouts  5.65 us
    ppermute x5, starting transfers between devices, right(): return lax.ppermute(x, 'ab', [(i, (i + 1) % GROUPS) for i in range(GROUPS)])  3.91 us
  transfers between devices with their start and end apart: 13, of which 10 were waited for; matrix products, arithmetic and copies ran while one was open for 0% of the time, Pallas kernels for 16%

profile of v4, /device:TPU:32, one launch (start us, length us, event | category | flops | bytes accessed | tf_op | source)
XLA Modules:
  0.0 86.0 jit_solution(1784301133488494697)
XLA Ops:
  0.0 1.1 %slice_bitcast_fusion = (f32[32,1792]{1,0:T(8,128)S(1)}, f32[32,1792]{1,0:T(8,128)S(1)}) fusion(f32[2,32,7168]{2,1,0:T(8,128)} %own_ref.3), kind=kLoop, calls=%fused_computation | loop fusion | bytes 917504 | tf_op jit(solution)/shard_map/squeeze | solution.py:222
  1.1 1.6 %collective-permute-start = (f32[32,1792]{1,0:T(8,128)S(1)}, f32[32,1792]{1,0:T(8,128)S(1)}, u32[]{:S(2)}, u32[]{:S(2)}) collective-permute-start(f32[32,1792]{1,0:T(8,128)S(1)} %get-tuple-element.24), channel_id=1, source_target_pairs={{0,1},{1,2},{2,3},{3,0},{4,5},{5,6},{6,7},{7,4},{8,9},{9,10},{10,1... | collective-permute-start | bytes 688136 | tf_op jit(solution)/shard_map/ppermute | solution.py:204
  2.7 1.7 %collective-permute-start.1 = (f32[32,1792]{1,0:T(8,128)S(1)}, f32[32,1792]{1,0:T(8,128)S(1)}, u32[]{:S(2)}, u32[]{:S(2)}) collective-permute-start(f32[32,1792]{1,0:T(8,128)S(1)} %get-tuple-element.23), channel_id=1, source_target_pairs={{0,3},{1,0},{2,1},{3,2},{4,7},{5,4},{6,5},{7,6},{8,11},{9,8},{10,9... | collective-permute-start | bytes 688136 | tf_op jit(solution)/shard_map/ppermute | solution.py:208
  4.4 1.5 %copy-done.2 = f32[2,32,7168]{2,1,0:T(8,128)S(1)} copy-done((f32[2,32,7168]{2,1,0:T(8,128)S(1)}, f32[2,32,7168]{2,1,0:T(8,128)}, u32[]{:S(2)}) %copy-start.2) | copy-done | bytes 1835032
  5.9 0.4 shard_map.66
  6.3 0.4 collective-permute-start.2
  6.6 3.0 %collective-permute-start.3 = (f32[32,5376]{1,0:T(8,128)S(1)}, f32[32,5376]{1,0:T(8,128)S(1)}, u32[]{:S(2)}, u32[]{:S(2)}) collective-permute-start(f32[32,5376]{1,0:T(8,128)S(1)} %get-tuple-element.14), channel_id=1, source_target_pairs={{0,3},{1,0},{2,1},{3,2},{4,7},{5,4},{6,5},{7,6},{8,11},{9,8},{10,9... | collective-permute-start | bytes 2064392 | tf_op jit(solution)/shard_map/ppermute | solution.py:208
  9.7 0.3 collective-permute-done.refs_4_.refs_0_
  10.0 1.1 %collective-permute-done.1.refs_5_.refs_1_ = f32[32,1792]{1,0:T(8,128)S(1)} collective-permute-done((f32[32,1792]{1,0:T(8,128)S(1)}, f32[32,1792]{1,0:T(8,128)S(1)}, u32[]{:S(2)}, u32[]{:S(2)}) %collective-permute-start.1) | collective-permute-done | bytes 229408 | tf_op jit(solution)/shard_map/ppermute | solution.py:208
  11.1 4.1 %copy-done = f32[7168,384]{1,0:T(8,128)S(1)} copy-done((f32[7168,384]{1,0:T(8,128)S(1)}, f32[7168,384]{1,0:T(8,128)}, u32[]{:S(2)}) %copy-start) | copy-done | bytes 11010072
  15.2 3.5 %shard_map.64.refs_0_.own_ref = f32[64,384]{1,0:T(8,128)S(1)} custom-call(f32[2,32,7168]{2,1,0:T(8,128)S(1)} %copy-done.2, f32[2,32,7168]{2,1,0:T(8,128)S(1)} %copy-done.2, f32[2,7168]{1,0:T(2,128)S(1)} %pad_maximum_fusion.refs_2_, f32[7168,384]{1,0:T(8,128)S(1)} %copy-done, f32[32,1792]{1,0:T(8,128)S(1)} %collective-permute-done.refs_4_.refs_0_, ...), custom_call_target="tpu_custom_call" | custom-call | tf_op jit(solution)/shard_map/pallas_call | solution.py:60
  18.7 0.5 shard_map.68
  19.2 1.7 %collective-permute-start.4 = (f32[32,7168]{1,0:T(8,128)S(1)}, f32[32,7168]{1,0:T(8,128)S(1)}, u32[]{:S(2)}, u32[]{:S(2)}) collective-permute-start(f32[32,7168]{1,0:T(8,128)S(1)} %get-tuple-element.15), channel_id=1, source_target_pairs={{0,1},{1,2},{2,3},{3,0},{4,5},{5,6},{6,7},{7,4},{8,9},{9,10},{10,1... | collective-permute-start | bytes 2752520 | tf_op jit(solution)/shard_map/ppermute | solution.py:204
  20.9 1.6 %collective-permute-start.5 = (f32[32,7168]{1,0:T(8,128)S(1)}, f32[32,7168]{1,0:T(8,128)S(1)}, u32[]{:S(2)}, u32[]{:S(2)}) collective-permute-start(f32[32,7168]{1,0:T(8,128)S(1)} %get-tuple-element.16), channel_id=1, source_target_pairs={{0,3},{1,0},{2,1},{3,2},{4,7},{5,4},{6,5},{7,6},{8,11},{9,8},{10,9... | collective-permute-start | bytes 2752520 | tf_op jit(solution)/shard_map/ppermute | solution.py:208
  22.5 3.3 %collective-permute-done.3.refs_1_ = f32[32,5376]{1,0:T(8,128)S(1)} collective-permute-done((f32[32,5376]{1,0:T(8,128)S(1)}, f32[32,5376]{1,0:T(8,128)S(1)}, u32[]{:S(2)}, u32[]{:S(2)}) %collective-permute-start.3) | collective-permute-done | bytes 688160 | tf_op jit(solution)/shard_map/ppermute | solution.py:208
  25.8 3.3 %collective-permute-start.10 = (f32[32,5376]{1,0:T(8,128)S(1)}, f32[32,5376]{1,0:T(8,128)S(1)}, u32[]{:S(2)}, u32[]{:S(2)}) collective-permute-start(f32[32,5376]{1,0:T(8,128)S(1)} %collective-permute-done.3.refs_1_), channel_id=1, source_target_pairs={{0,3},{1,0},{2,1},{3,2},{4,7},{5,4},{6,5},{7,6},{8,11},{9,8},{10,9... | collective-permute-start | bytes 2064392 | tf_op jit(solution)/shard_map/ppermute | solution.py:208
  29.2 0.3 collective-permute-start.7
  29.5 16.1 %collective-permute-done.4.refs_0_ = f32[32,7168]{1,0:T(8,128)S(1)} collective-permute-done((f32[32,7168]{1,0:T(8,128)S(1)}, f32[32,7168]{1,0:T(8,128)S(1)}, u32[]{:S(2)}, u32[]{:S(2)}) %collective-permute-start.4) | collective-permute-done | bytes 917536 | tf_op jit(solution)/shard_map/ppermute | solution.py:204
  45.6 1.2 %collective-permute-start.8 = (f32[32,1792]{1,0:T(8,128)S(1)}, f32[32,1792]{1,0:T(8,128)S(1)}, u32[]{:S(2)}, u32[]{:S(2)}) collective-permute-start(f32[32,1792]{1,0:T(8,128)S(1)} %collective-permute-done.1.refs_5_.refs_1_), channel_id=1, source_target_pairs={{0,3},{1,0},{2,1},{3,2},{4,7},{5,4},{6,5},{7,6},{8,11},{9,8},{10,9... | collective-permute-start | bytes 688136 | tf_op jit(solution)/shard_map/ppermute | solution.py:208
  46.8 0.8 shard_map.65
  47.7 2.7 %shard_map.67 = f32[64,384]{1,0:T(8,128)S(1)} custom-call(f32[32,5376]{1,0:T(8,128)S(1)} %collective-permute-done.2.refs_0_, f32[32,5376]{1,0:T(8,128)S(1)} %collective-permute-done.3.refs_1_, f32[2,7168]{1,0:T(2,128)S(1)} %pad_maximum_fusion.refs_2_, f32[7168,384]{1,0:T(8,128)S(1)} %copy-done.1), custom_call_target="tpu_custom_call" | custom-call | tf_op jit(solution)/shard_map/pallas_call | solution.py:74
  50.4 3.5 %shard_map.69.far_ref = f32[64,384]{1,0:T(8,128)S(1)} custom-call(f32[32,7168]{1,0:T(8,128)S(1)} %collective-permute-done.4.refs_0_, f32[32,7168]{1,0:T(8,128)S(1)} %collective-permute-done.5.refs_1_, f32[2,7168]{1,0:T(2,128)S(1)} %pad_maximum_fusion.refs_2_, f32[7168,384]{1,0:T(8,128)S(1)} %copy-done.1), custom_call_target="tpu_custom_call" | custom-call | tf_op jit(solution)/shard_map/pallas_call | solution.py:74
  54.3 1.4 %collective-permute-done.6.refs_4_.got_ref = f32[32,4,384]{2,1,0:T(4,128)S(1)} collective-permute-done((f32[32,4,384]{2,1,0:T(4,128)S(1)}, f32[32,4,384]{2,1,0:T(4,128)S(1)}, u32[]{:S(2)}, u32[]{:S(2)}) %collective-permute-start.6) | collective-permute-done | bytes 196640 | tf_op jit(solution)/shard_map/ppermute | solution.py:212
  55.7 4.5 %collective-permute-done.10.refs_1_ = f32[32,5376]{1,0:T(8,128)S(1)} collective-permute-done((f32[32,5376]{1,0:T(8,128)S(1)}, f32[32,5376]{1,0:T(8,128)S(1)}, u32[]{:S(2)}, u32[]{:S(2)}) %collective-permute-start.10) | collective-permute-done | bytes 688160 | tf_op jit(solution)/shard_map/ppermute | solution.py:208
  60.3 2.6 %shard_map.71.refs_4_ = f32[64,384]{1,0:T(8,128)S(1)} custom-call(f32[32,5376]{1,0:T(8,128)S(1)} %collective-permute-done.9.refs_0_, f32[32,5376]{1,0:T(8,128)S(1)} %collective-permute-done.10.refs_1_, f32[2,7168]{1,0:T(2,128)S(1)} %pad_maximum_fusion.refs_2_, f32[7168,384]{1,0:T(8,128)S(1)} %copy-done.1, ...), custom_call_target="tpu_custom_call" | custom-call | tf_op jit(solution)/shard_map/pallas_call | solution.py:74
  63.0 0.8 collective-permute-done.7.refs_0_
  63.8 0.9 %shard_map.72 = (f32[8,4,384]{2,1,0:T(4,128)S(1)}, f32[8,4,384]{2,1,0:T(4,128)S(1)}) custom-call(f32[32,1792]{1,0:T(8,128)S(1)} %collective-permute-done.7.refs_0_, f32[32,1792]{1,0:T(8,128)S(1)} %collective-permute-done.8.refs_1_, f32[2,7168]{1,0:T(2,128)S(1)} %pad_maximum_fusion.refs_2_, f32[7168,384]{1,0:T(8,128)S(1)} %copy-done.1, ...), custom_call_target="tpu_custom_call" | custom-call | tf_op jit(solution)/shard_map/pallas_call | solution.py:148
  64.8 1.2 %collective-permute-done.11.got_opposite_ref = f32[8,4,384]{2,1,0:T(4,128)S(1)} collective-permute-done((f32[8,4,384]{2,1,0:T(4,128)S(1)}, f32[8,4,384]{2,1,0:T(4,128)S(1)}, u32[]{:S(2)}, u32[]{:S(2)}) %collective-permute-start.11) | collective-permute-done | bytes 49184 | tf_op jit(solution)/shard_map/ppermute | solution.py:212
  66.0 0.7 shard_map.73
  66.7 12.4 %all-to-all-start = ((f32[32,4,384]{2,1,0:T(4,128)}), f32[32,4,384]{2,1,0:T(4,128)S(1)}, u32[]{:S(2)}, u32[]{:S(2)}) async-start(f32[32,4,384]{2,1,0:T(4,128)} %shard_map.73), calls=%async_computation | async-start | bytes 393216 | tf_op jit(solution)/shard_map/all_to_all | solution.py:243
  79.1 6.2 %all-to-all-done.shares_ref = f32[32,4,384]{2,1,0:T(4,128)S(1)} async-done(((f32[32,4,384]{2,1,0:T(4,128)}), f32[32,4,384]{2,1,0:T(4,128)S(1)}, u32[]{:S(2)}, u32[]{:S(2)}) %all-to-all-start) | async-done | bytes 196640 | tf_op jit(solution)/shard_map/all_to_all | solution.py:243
  85.3 0.6 shard_map.74
  (26 shorter events, 0.7 us)
Async XLA Ops:
  0.0 9.6 %copy-start.3 = (s32[7168]{0:T(1024)S(1)}, s32[7168]{0:T(1024)}, u32[]{:S(2)}) copy-start(s32[7168]{0:T(1024)} %param.8) | copy-start | bytes 86020
  0.0 9.6 %copy-start.4 = (s32[7168]{0:T(1024)S(1)}, s32[7168]{0:T(1024)}, u32[]{:S(2)}) copy-start(s32[7168]{0:T(1024)} %param.9) | copy-start | bytes 86020
  1.1 8.9 %collective-permute-start = (f32[32,1792]{1,0:T(8,128)S(1)}, f32[32,1792]{1,0:T(8,128)S(1)}, u32[]{:S(2)}, u32[]{:S(2)}) collective-permute-start(f32[32,1792]{1,0:T(8,128)S(1)} %get-tuple-element.24), channel_id=1, source_target_pairs={{0,1},{1,2},{2,3},{3,0},{4,5},{5,6},{6,7},{7,4},{8,9},{9,10},{10,1... | collective-permute-start | bytes 688136 | tf_op jit(solution)/shard_map/ppermute | solution.py:204
  2.7 8.4 %collective-permute-start.1 = (f32[32,1792]{1,0:T(8,128)S(1)}, f32[32,1792]{1,0:T(8,128)S(1)}, u32[]{:S(2)}, u32[]{:S(2)}) collective-permute-start(f32[32,1792]{1,0:T(8,128)S(1)} %get-tuple-element.23), channel_id=1, source_target_pairs={{0,3},{1,0},{2,1},{3,2},{4,7},{5,4},{6,5},{7,6},{8,11},{9,8},{10,9... | collective-permute-start | bytes 688136 | tf_op jit(solution)/shard_map/ppermute | solution.py:208
  4.4 1.5 %copy-start.2 = (f32[2,32,7168]{2,1,0:T(8,128)S(1)}, f32[2,32,7168]{2,1,0:T(8,128)}, u32[]{:S(2)}) copy-start(f32[2,32,7168]{2,1,0:T(8,128)} %own_ref.3) | copy-start | bytes 5505028
  6.3 22.9 %collective-permute-start.2 = (f32[32,5376]{1,0:T(8,128)S(1)}, f32[32,5376]{1,0:T(8,128)S(1)}, u32[]{:S(2)}, u32[]{:S(2)}) collective-permute-start(f32[32,5376]{1,0:T(8,128)S(1)} %get-tuple-element.13), channel_id=1, source_target_pairs={{0,1},{1,2},{2,3},{3,0},{4,5},{5,6},{6,7},{7,4},{8,9},{9,10},{10,1... | collective-permute-start | bytes 2064392 | tf_op jit(solution)/shard_map/ppermute | solution.py:204
  6.6 19.2 %collective-permute-start.3 = (f32[32,5376]{1,0:T(8,128)S(1)}, f32[32,5376]{1,0:T(8,128)S(1)}, u32[]{:S(2)}, u32[]{:S(2)}) collective-permute-start(f32[32,5376]{1,0:T(8,128)S(1)} %get-tuple-element.14), channel_id=1, source_target_pairs={{0,3},{1,0},{2,1},{3,2},{4,7},{5,4},{6,5},{7,6},{8,11},{9,8},{10,9... | collective-permute-start | bytes 2064392 | tf_op jit(solution)/shard_map/ppermute | solution.py:208
  11.1 4.1 %copy-start = (f32[7168,384]{1,0:T(8,128)S(1)}, f32[7168,384]{1,0:T(8,128)}, u32[]{:S(2)}) copy-start(f32[7168,384]{1,0:T(8,128)} %refs_3_.11) | copy-start | bytes 33030148
  15.2 31.6 %copy-start.1 = (f32[7168,384]{1,0:T(8,128)S(1)}, f32[7168,384]{1,0:T(8,128)}, u32[]{:S(2)}) copy-start(f32[7168,384]{1,0:T(8,128)} %refs_3_.11) | copy-start | bytes 33030148
  19.2 26.4 %collective-permute-start.4 = (f32[32,7168]{1,0:T(8,128)S(1)}, f32[32,7168]{1,0:T(8,128)S(1)}, u32[]{:S(2)}, u32[]{:S(2)}) collective-permute-start(f32[32,7168]{1,0:T(8,128)S(1)} %get-tuple-element.15), channel_id=1, source_target_pairs={{0,1},{1,2},{2,3},{3,0},{4,5},{5,6},{6,7},{7,4},{8,9},{9,10},{10,1... | collective-permute-start | bytes 2752520 | tf_op jit(solution)/shard_map/ppermute | solution.py:204
  20.9 29.4 %collective-permute-start.5 = (f32[32,7168]{1,0:T(8,128)S(1)}, f32[32,7168]{1,0:T(8,128)S(1)}, u32[]{:S(2)}, u32[]{:S(2)}) collective-permute-start(f32[32,7168]{1,0:T(8,128)S(1)} %get-tuple-element.16), channel_id=1, source_target_pairs={{0,3},{1,0},{2,1},{3,2},{4,7},{5,4},{6,5},{7,6},{8,11},{9,8},{10,9... | collective-permute-start | bytes 2752520 | tf_op jit(solution)/shard_map/ppermute | solution.py:208
  25.8 34.4 %collective-permute-start.10 = (f32[32,5376]{1,0:T(8,128)S(1)}, f32[32,5376]{1,0:T(8,128)S(1)}, u32[]{:S(2)}, u32[]{:S(2)}) collective-permute-start(f32[32,5376]{1,0:T(8,128)S(1)} %collective-permute-done.3.refs_1_), channel_id=1, source_target_pairs={{0,3},{1,0},{2,1},{3,2},{4,7},{5,4},{6,5},{7,6},{8,11},{9,8},{10,9... | collective-permute-start | bytes 2064392 | tf_op jit(solution)/shard_map/ppermute | solution.py:208
  29.2 31.2 %collective-permute-start.9 = (f32[32,5376]{1,0:T(8,128)S(1)}, f32[32,5376]{1,0:T(8,128)S(1)}, u32[]{:S(2)}, u32[]{:S(2)}) collective-permute-start(f32[32,5376]{1,0:T(8,128)S(1)} %collective-permute-done.2.refs_0_), channel_id=1, source_target_pairs={{0,1},{1,2},{2,3},{3,0},{4,5},{5,6},{6,7},{7,4},{8,9},{9,10},{10,1... | collective-permute-start | bytes 2064392 | tf_op jit(solution)/shard_map/ppermute | solution.py:204
  29.2 34.6 %collective-permute-start.7 = (f32[32,1792]{1,0:T(8,128)S(1)}, f32[32,1792]{1,0:T(8,128)S(1)}, u32[]{:S(2)}, u32[]{:S(2)}) collective-permute-start(f32[32,1792]{1,0:T(8,128)S(1)} %collective-permute-done.refs_4_.refs_0_), channel_id=1, source_target_pairs={{0,1},{1,2},{2,3},{3,0},{4,5},{5,6},{6,7},{7,4},{8,9},{9,10},{10,1... | collective-permute-start | bytes 688136 | tf_op jit(solution)/shard_map/ppermute | solution.py:204
  45.6 18.2 %collective-permute-start.8 = (f32[32,1792]{1,0:T(8,128)S(1)}, f32[32,1792]{1,0:T(8,128)S(1)}, u32[]{:S(2)}, u32[]{:S(2)}) collective-permute-start(f32[32,1792]{1,0:T(8,128)S(1)} %collective-permute-done.1.refs_5_.refs_1_), channel_id=1, source_target_pairs={{0,3},{1,0},{2,1},{3,2},{4,7},{5,4},{6,5},{7,6},{8,11},{9,8},{10,9... | collective-permute-start | bytes 688136 | tf_op jit(solution)/shard_map/ppermute | solution.py:208
  54.0 1.7 %collective-permute-start.6 = (f32[32,4,384]{2,1,0:T(4,128)S(1)}, f32[32,4,384]{2,1,0:T(4,128)S(1)}, u32[]{:S(2)}, u32[]{:S(2)}) collective-permute-start(f32[32,4,384]{2,1,0:T(4,128)S(1)} %get-tuple-element.18), channel_id=1, source_target_pairs={{0,4},{4,0},{8,12},{12,8},{16,20},{20,16},{24,28},{28,24},{32,36},... | collective-permute-start | bytes 589832 | tf_op jit(solution)/shard_map/ppermute | solution.py:212
  63.0 16.1 %copy-start.5 = (s32[384]{0:T(512)S(1)}, s32[384]{0:T(512)}, u32[]{:S(2)}) copy-start(s32[384]{0:T(512)} %param.10) | copy-start | bytes 4612
  63.0 16.1 %copy-start.6 = (s32[384]{0:T(512)S(1)}, s32[384]{0:T(512)}, u32[]{:S(2)}) copy-start(s32[384]{0:T(512)} %param.11) | copy-start | bytes 4612
  64.7 1.3 %collective-permute-start.11 = (f32[8,4,384]{2,1,0:T(4,128)S(1)}, f32[8,4,384]{2,1,0:T(4,128)S(1)}, u32[]{:S(2)}, u32[]{:S(2)}) collective-permute-start(f32[8,4,384]{2,1,0:T(4,128)S(1)} %get-tuple-element.20), channel_id=1, source_target_pairs={{0,4},{4,0},{8,12},{12,8},{16,20},{20,16},{24,28},{28,24},{32,36},... | collective-permute-start | bytes 147464 | tf_op jit(solution)/shard_map/ppermute | solution.py:212
  66.7 18.6 %all-to-all-start = ((f32[32,4,384]{2,1,0:T(4,128)}), f32[32,4,384]{2,1,0:T(4,128)S(1)}, u32[]{:S(2)}, u32[]{:S(2)}) async-start(f32[32,4,384]{2,1,0:T(4,128)} %shard_map.73), calls=%async_computation | async-start | bytes 393216 | tf_op jit(solution)/shard_map/all_to_all | solution.py:243

commit v5 on v4

--- a/solution.py
+++ b/solution.py
@@ -10,6 +10,7 @@
 F32 = jnp.float32
 BF16 = jnp.bfloat16
 STEP = 1792
+TAIL = 896
 VMEM = pltpu.CompilerParams(vmem_limit_bytes=24 * 2**20)
 FREE = pl.CostEstimate(flops=0, bytes_accessed=0, transcendentals=0)
 GROUPS, LAYERS, CORES = 4, 8, 2
@@ -46,10 +47,10 @@
     add_step(slabs, refs[:n], refs[n], refs[n + 1], total_ref)
 
 
-def specs(piece_specs, columns, first):
+def specs(piece_specs, columns, first, step=STEP):
     return piece_specs + [
-        pl.BlockSpec((2, STEP), lambda k: (0, k + first)),
-        pl.BlockSpec((STEP, columns), lambda k: (k + first, 0)),
+        pl.BlockSpec((2, step), lambda k: (0, k + first)),
+        pl.BlockSpec((step, columns), lambda k: (k + first, 0)),
     ]
 
 
@@ -147,8 +148,8 @@
     columns = integrals.shape[1]
     return pl.pallas_call(
         functools.partial(opposite_kernel, slabs),
-        grid=(pairs // STEP,),
-        in_specs=specs([pl.BlockSpec((rows, STEP), lambda k: (0, k))] * n, columns, first)
+        grid=(pairs // TAIL,),
+        in_specs=specs([pl.BlockSpec((rows, TAIL), lambda k: (0, k))] * n, columns, first, TAIL)
         + [pl.BlockSpec(before.shape, lambda k: (0, 0))],
         out_specs=[pl.BlockSpec((LAYERS, 4, columns), lambda k: (0, 0, 0))] * 2,
         out_shape=[jax.ShapeDtypeStruct((LAYERS, 4, columns), F32)] * 2,
@@ -234,7 +235,7 @@
     mine, other = exchange(own, near, far)
     got = over_cores(other)
     opposite = partial_sums(onward, (0, 1), weights, integrals, 0, (got,))
-    mine_opposite, other = opposite_sums(onward_last, (0, 1), weights, integrals, cut // STEP, opposite)
+    mine_opposite, other = opposite_sums(onward_last, (0, 1), weights, integrals, cut // TAIL, opposite)
     part_sum = last_sums(mine, got, mine_opposite, over_cores(other))
 
     planes = [

time: 87.3 us -> 87.4 us (level)
  no operation moved by 1% of the time
where the time goes in v5:
time: 87.4 us; the launch traced here: 86.1 us
  waiting for transfers between devices  35.3 us (40%)
  starting transfers between devices  27.3 us (31%)
  Pallas kernels  16.5 us (19%)
  local copies, waits for them, and re-layouts  6.74 us (8%)
    ppermute x5, waiting for transfers between devices, right(): return lax.ppermute(x, 'ab', [(i, (i + 1) % GROUPS) for i in range(GROUPS)])  17.3 us
    all_to_all x1, starting transfers between devices, local(): lax.all_to_all(part_sum, 'cd', 0, 0, tiled=True, axis_index_groups=planes)  12.4 us
    ppermute x5, starting transfers between devices, left(): return lax.ppermute(x, 'ab', [(i, (i - 1) % GROUPS) for i in range(GROUPS)])  10.9 us
    pallas_call x4, Pallas kernels, partial_sums(): pl.pallas_call(functools.partial(sum_kernel, slabs), grid=(pairs // STEP,...  9.64 us
    ppermute x5, waiting for transfers between devices, left(): return lax.ppermute(x, 'ab', [(i, (i - 1) % GROUPS) for i in range(GROUPS)])  9.11 us
    all_to_all x1, waiting for transfers between devices, local(): lax.all_to_all(part_sum, 'cd', 0, 0, tiled=True, axis_index_groups=planes)  6.24 us
    unnamed x14, local copies, waits for them, and re-layouts  5.65 us
    ppermute x5, starting transfers between devices, right(): return lax.ppermute(x, 'ab', [(i, (i + 1) % GROUPS) for i in range(GROUPS)])  3.88 us
  transfers between devices with their start and end apart: 13, of which 10 were waited for; matrix products, arithmetic and copies ran while one was open for 0% of the time, Pallas kernels for 16%

profile of v5, /device:TPU:32, one launch (start us, length us, event | category | flops | bytes accessed | tf_op | source)
XLA Modules:
  0.0 86.1 jit_solution(10988587908219947768)
XLA Ops:
  0.0 1.1 %slice_bitcast_fusion = (f32[32,1792]{1,0:T(8,128)S(1)}, f32[32,1792]{1,0:T(8,128)S(1)}) fusion(f32[2,32,7168]{2,1,0:T(8,128)} %own_ref.3), kind=kLoop, calls=%fused_computation | loop fusion | bytes 917504 | tf_op jit(solution)/shard_map/squeeze | solution.py:223
  1.1 1.6 %collective-permute-start = (f32[32,1792]{1,0:T(8,128)S(1)}, f32[32,1792]{1,0:T(8,128)S(1)}, u32[]{:S(2)}, u32[]{:S(2)}) collective-permute-start(f32[32,1792]{1,0:T(8,128)S(1)} %get-tuple-element.24), channel_id=1, source_target_pairs={{0,1},{1,2},{2,3},{3,0},{4,5},{5,6},{6,7},{7,4},{8,9},{9,10},{10,1... | collective-permute-start | bytes 688136 | tf_op jit(solution)/shard_map/ppermute | solution.py:205
  2.7 1.7 %collective-permute-start.1 = (f32[32,1792]{1,0:T(8,128)S(1)}, f32[32,1792]{1,0:T(8,128)S(1)}, u32[]{:S(2)}, u32[]{:S(2)}) collective-permute-start(f32[32,1792]{1,0:T(8,128)S(1)} %get-tuple-element.23), channel_id=1, source_target_pairs={{0,3},{1,0},{2,1},{3,2},{4,7},{5,4},{6,5},{7,6},{8,11},{9,8},{10,9... | collective-permute-start | bytes 688136 | tf_op jit(solution)/shard_map/ppermute | solution.py:209
  4.4 1.5 %copy-done.2 = f32[2,32,7168]{2,1,0:T(8,128)S(1)} copy-done((f32[2,32,7168]{2,1,0:T(8,128)S(1)}, f32[2,32,7168]{2,1,0:T(8,128)}, u32[]{:S(2)}) %copy-start.2) | copy-done | bytes 1835032
  5.9 0.4 shard_map.66
  6.3 0.4 collective-permute-start.2
  6.6 3.0 %collective-permute-start.3 = (f32[32,5376]{1,0:T(8,128)S(1)}, f32[32,5376]{1,0:T(8,128)S(1)}, u32[]{:S(2)}, u32[]{:S(2)}) collective-permute-start(f32[32,5376]{1,0:T(8,128)S(1)} %get-tuple-element.14), channel_id=1, source_target_pairs={{0,3},{1,0},{2,1},{3,2},{4,7},{5,4},{6,5},{7,6},{8,11},{9,8},{10,9... | collective-permute-start | bytes 2064392 | tf_op jit(solution)/shard_map/ppermute | solution.py:209
  9.7 0.3 collective-permute-done.refs_4_.refs_0_
  10.0 1.1 %collective-permute-done.1.refs_5_.refs_1_ = f32[32,1792]{1,0:T(8,128)S(1)} collective-permute-done((f32[32,1792]{1,0:T(8,128)S(1)}, f32[32,1792]{1,0:T(8,128)S(1)}, u32[]{:S(2)}, u32[]{:S(2)}) %collective-permute-start.1) | collective-permute-done | bytes 229408 | tf_op jit(solution)/shard_map/ppermute | solution.py:209
  11.1 4.1 %copy-done = f32[7168,384]{1,0:T(8,128)S(1)} copy-done((f32[7168,384]{1,0:T(8,128)S(1)}, f32[7168,384]{1,0:T(8,128)}, u32[]{:S(2)}) %copy-start) | copy-done | bytes 11010072
  15.2 3.5 %shard_map.64.refs_0_.own_ref = f32[64,384]{1,0:T(8,128)S(1)} custom-call(f32[2,32,7168]{2,1,0:T(8,128)S(1)} %copy-done.2, f32[2,32,7168]{2,1,0:T(8,128)S(1)} %copy-done.2, f32[2,7168]{1,0:T(2,128)S(1)} %pad_maximum_fusion.refs_2_, f32[7168,384]{1,0:T(8,128)S(1)} %copy-done, f32[32,1792]{1,0:T(8,128)S(1)} %collective-permute-done.refs_4_.refs_0_, ...), custom_call_target="tpu_custom_call" | custom-call | tf_op jit(solution)/shard_map/pallas_call | solution.py:61
  18.7 0.5 shard_map.68
  19.2 1.7 %collective-permute-start.4 = (f32[32,7168]{1,0:T(8,128)S(1)}, f32[32,7168]{1,0:T(8,128)S(1)}, u32[]{:S(2)}, u32[]{:S(2)}) collective-permute-start(f32[32,7168]{1,0:T(8,128)S(1)} %get-tuple-element.15), channel_id=1, source_target_pairs={{0,1},{1,2},{2,3},{3,0},{4,5},{5,6},{6,7},{7,4},{8,9},{9,10},{10,1... | collective-permute-start | bytes 2752520 | tf_op jit(solution)/shard_map/ppermute | solution.py:205
  20.9 1.6 %collective-permute-start.5 = (f32[32,7168]{1,0:T(8,128)S(1)}, f32[32,7168]{1,0:T(8,128)S(1)}, u32[]{:S(2)}, u32[]{:S(2)}) collective-permute-start(f32[32,7168]{1,0:T(8,128)S(1)} %get-tuple-element.16), channel_id=1, source_target_pairs={{0,3},{1,0},{2,1},{3,2},{4,7},{5,4},{6,5},{7,6},{8,11},{9,8},{10,9... | collective-permute-start | bytes 2752520 | tf_op jit(solution)/shard_map/ppermute | solution.py:209
  22.5 3.3 %collective-permute-done.3.refs_1_ = f32[32,5376]{1,0:T(8,128)S(1)} collective-permute-done((f32[32,5376]{1,0:T(8,128)S(1)}, f32[32,5376]{1,0:T(8,128)S(1)}, u32[]{:S(2)}, u32[]{:S(2)}) %collective-permute-start.3) | collective-permute-done | bytes 688160 | tf_op jit(solution)/shard_map/ppermute | solution.py:209
  25.8 3.3 %collective-permute-start.10 = (f32[32,5376]{1,0:T(8,128)S(1)}, f32[32,5376]{1,0:T(8,128)S(1)}, u32[]{:S(2)}, u32[]{:S(2)}) collective-permute-start(f32[32,5376]{1,0:T(8,128)S(1)} %collective-permute-done.3.refs_1_), channel_id=1, source_target_pairs={{0,3},{1,0},{2,1},{3,2},{4,7},{5,4},{6,5},{7,6},{8,11},{9,8},{10,9... | collective-permute-start | bytes 2064392 | tf_op jit(solution)/shard_map/ppermute | solution.py:209
  29.2 0.3 collective-permute-start.7
  29.5 16.1 %collective-permute-done.4.refs_0_ = f32[32,7168]{1,0:T(8,128)S(1)} collective-permute-done((f32[32,7168]{1,0:T(8,128)S(1)}, f32[32,7168]{1,0:T(8,128)S(1)}, u32[]{:S(2)}, u32[]{:S(2)}) %collective-permute-start.4) | collective-permute-done | bytes 917536 | tf_op jit(solution)/shard_map/ppermute | solution.py:205
  45.6 1.2 %collective-permute-start.8 = (f32[32,1792]{1,0:T(8,128)S(1)}, f32[32,1792]{1,0:T(8,128)S(1)}, u32[]{:S(2)}, u32[]{:S(2)}) collective-permute-start(f32[32,1792]{1,0:T(8,128)S(1)} %collective-permute-done.1.refs_5_.refs_1_), channel_id=1, source_target_pairs={{0,3},{1,0},{2,1},{3,2},{4,7},{5,4},{6,5},{7,6},{8,11},{9,8},{10,9... | collective-permute-start | bytes 688136 | tf_op jit(solution)/shard_map/ppermute | solution.py:209
  46.8 0.8 shard_map.65
  47.7 2.7 %shard_map.67 = f32[64,384]{1,0:T(8,128)S(1)} custom-call(f32[32,5376]{1,0:T(8,128)S(1)} %collective-permute-done.2.refs_0_, f32[32,5376]{1,0:T(8,128)S(1)} %collective-permute-done.3.refs_1_, f32[2,7168]{1,0:T(2,128)S(1)} %pad_maximum_fusion.refs_2_, f32[7168,384]{1,0:T(8,128)S(1)} %copy-done.1), custom_call_target="tpu_custom_call" | custom-call | tf_op jit(solution)/shard_map/pallas_call | solution.py:75
  50.3 3.5 %shard_map.69.far_ref = f32[64,384]{1,0:T(8,128)S(1)} custom-call(f32[32,7168]{1,0:T(8,128)S(1)} %collective-permute-done.4.refs_0_, f32[32,7168]{1,0:T(8,128)S(1)} %collective-permute-done.5.refs_1_, f32[2,7168]{1,0:T(2,128)S(1)} %pad_maximum_fusion.refs_2_, f32[7168,384]{1,0:T(8,128)S(1)} %copy-done.1), custom_call_target="tpu_custom_call" | custom-call | tf_op jit(solution)/shard_map/pallas_call | solution.py:75
  54.1 1.4 %collective-permute-done.6.refs_4_.got_ref = f32[32,4,384]{2,1,0:T(4,128)S(1)} collective-permute-done((f32[32,4,384]{2,1,0:T(4,128)S(1)}, f32[32,4,384]{2,1,0:T(4,128)S(1)}, u32[]{:S(2)}, u32[]{:S(2)}) %collective-permute-start.6) | collective-permute-done | bytes 196640 | tf_op jit(solution)/shard_map/ppermute | solution.py:213
  55.5 4.7 %collective-permute-done.10.refs_1_ = f32[32,5376]{1,0:T(8,128)S(1)} collective-permute-done((f32[32,5376]{1,0:T(8,128)S(1)}, f32[32,5376]{1,0:T(8,128)S(1)}, u32[]{:S(2)}, u32[]{:S(2)}) %collective-permute-start.10) | collective-permute-done | bytes 688160 | tf_op jit(solution)/shard_map/ppermute | solution.py:209
  60.3 2.6 %shard_map.71.refs_4_ = f32[64,384]{1,0:T(8,128)S(1)} custom-call(f32[32,5376]{1,0:T(8,128)S(1)} %collective-permute-done.9.refs_0_, f32[32,5376]{1,0:T(8,128)S(1)} %collective-permute-done.10.refs_1_, f32[2,7168]{1,0:T(2,128)S(1)} %pad_maximum_fusion.refs_2_, f32[7168,384]{1,0:T(8,128)S(1)} %copy-done.1, ...), custom_call_target="tpu_custom_call" | custom-call | tf_op jit(solution)/shard_map/pallas_call | solution.py:75
  63.0 0.8 collective-permute-done.7.refs_0_
  63.8 1.0 %shard_map.72 = (f32[8,4,384]{2,1,0:T(4,128)S(1)}, f32[8,4,384]{2,1,0:T(4,128)S(1)}) custom-call(f32[32,1792]{1,0:T(8,128)S(1)} %collective-permute-done.7.refs_0_, f32[32,1792]{1,0:T(8,128)S(1)} %collective-permute-done.8.refs_1_, f32[2,7168]{1,0:T(2,128)S(1)} %pad_maximum_fusion.refs_2_, f32[7168,384]{1,0:T(8,128)S(1)} %copy-done.1, ...), custom_call_target="tpu_custom_call" | custom-call | tf_op jit(solution)/shard_map/pallas_call | solution.py:149
  64.9 1.2 %collective-permute-done.11.got_opposite_ref = f32[8,4,384]{2,1,0:T(4,128)S(1)} collective-permute-done((f32[8,4,384]{2,1,0:T(4,128)S(1)}, f32[8,4,384]{2,1,0:T(4,128)S(1)}, u32[]{:S(2)}, u32[]{:S(2)}) %collective-permute-start.11) | collective-permute-done | bytes 49184 | tf_op jit(solution)/shard_map/ppermute | solution.py:213
  66.1 0.7 shard_map.73
  66.8 12.4 %all-to-all-start = ((f32[32,4,384]{2,1,0:T(4,128)}), f32[32,4,384]{2,1,0:T(4,128)S(1)}, u32[]{:S(2)}, u32[]{:S(2)}) async-start(f32[32,4,384]{2,1,0:T(4,128)} %shard_map.73), calls=%async_computation | async-start | bytes 393216 | tf_op jit(solution)/shard_map/all_to_all | solution.py:244
  79.2 6.2 %all-to-all-done.shares_ref = f32[32,4,384]{2,1,0:T(4,128)S(1)} async-done(((f32[32,4,384]{2,1,0:T(4,128)}), f32[32,4,384]{2,1,0:T(4,128)S(1)}, u32[]{:S(2)}, u32[]{:S(2)}) %all-to-all-start) | async-done | bytes 196640 | tf_op jit(solution)/shard_map/all_to_all | solution.py:244
  85.5 0.6 shard_map.74
  (26 shorter events, 0.6 us)
Async XLA Ops:
  0.0 9.6 %copy-start.3 = (s32[7168]{0:T(1024)S(1)}, s32[7168]{0:T(1024)}, u32[]{:S(2)}) copy-start(s32[7168]{0:T(1024)} %param.8) | copy-start | bytes 86020
  0.0 9.6 %copy-start.4 = (s32[7168]{0:T(1024)S(1)}, s32[7168]{0:T(1024)}, u32[]{:S(2)}) copy-start(s32[7168]{0:T(1024)} %param.9) | copy-start | bytes 86020
  1.1 8.9 %collective-permute-start = (f32[32,1792]{1,0:T(8,128)S(1)}, f32[32,1792]{1,0:T(8,128)S(1)}, u32[]{:S(2)}, u32[]{:S(2)}) collective-permute-start(f32[32,1792]{1,0:T(8,128)S(1)} %get-tuple-element.24), channel_id=1, source_target_pairs={{0,1},{1,2},{2,3},{3,0},{4,5},{5,6},{6,7},{7,4},{8,9},{9,10},{10,1... | collective-permute-start | bytes 688136 | tf_op jit(solution)/shard_map/ppermute | solution.py:205
  2.7 8.4 %collective-permute-start.1 = (f32[32,1792]{1,0:T(8,128)S(1)}, f32[32,1792]{1,0:T(8,128)S(1)}, u32[]{:S(2)}, u32[]{:S(2)}) collective-permute-start(f32[32,1792]{1,0:T(8,128)S(1)} %get-tuple-element.23), channel_id=1, source_target_pairs={{0,3},{1,0},{2,1},{3,2},{4,7},{5,4},{6,5},{7,6},{8,11},{9,8},{10,9... | collective-permute-start | bytes 688136 | tf_op jit(solution)/shard_map/ppermute | solution.py:209
  4.4 1.5 %copy-start.2 = (f32[2,32,7168]{2,1,0:T(8,128)S(1)}, f32[2,32,7168]{2,1,0:T(8,128)}, u32[]{:S(2)}) copy-start(f32[2,32,7168]{2,1,0:T(8,128)} %own_ref.3) | copy-start | bytes 5505028
  6.3 22.9 %collective-permute-start.2 = (f32[32,5376]{1,0:T(8,128)S(1)}, f32[32,5376]{1,0:T(8,128)S(1)}, u32[]{:S(2)}, u32[]{:S(2)}) collective-permute-start(f32[32,5376]{1,0:T(8,128)S(1)} %get-tuple-element.13), channel_id=1, source_target_pairs={{0,1},{1,2},{2,3},{3,0},{4,5},{5,6},{6,7},{7,4},{8,9},{9,10},{10,1... | collective-permute-start | bytes 2064392 | tf_op jit(solution)/shard_map/ppermute | solution.py:205
  6.6 19.2 %collective-permute-start.3 = (f32[32,5376]{1,0:T(8,128)S(1)}, f32[32,5376]{1,0:T(8,128)S(1)}, u32[]{:S(2)}, u32[]{:S(2)}) collective-permute-start(f32[32,5376]{1,0:T(8,128)S(1)} %get-tuple-element.14), channel_id=1, source_target_pairs={{0,3},{1,0},{2,1},{3,2},{4,7},{5,4},{6,5},{7,6},{8,11},{9,8},{10,9... | collective-permute-start | bytes 2064392 | tf_op jit(solution)/shard_map/ppermute | solution.py:209
  11.1 4.1 %copy-start = (f32[7168,384]{1,0:T(8,128)S(1)}, f32[7168,384]{1,0:T(8,128)}, u32[]{:S(2)}) copy-start(f32[7168,384]{1,0:T(8,128)} %refs_3_.11) | copy-start | bytes 33030148
  15.2 31.6 %copy-start.1 = (f32[7168,384]{1,0:T(8,128)S(1)}, f32[7168,384]{1,0:T(8,128)}, u32[]{:S(2)}) copy-start(f32[7168,384]{1,0:T(8,128)} %refs_3_.11) | copy-start | bytes 33030148
  19.2 26.4 %collective-permute-start.4 = (f32[32,7168]{1,0:T(8,128)S(1)}, f32[32,7168]{1,0:T(8,128)S(1)}, u32[]{:S(2)}, u32[]{:S(2)}) collective-permute-start(f32[32,7168]{1,0:T(8,128)S(1)} %get-tuple-element.15), channel_id=1, source_target_pairs={{0,1},{1,2},{2,3},{3,0},{4,5},{5,6},{6,7},{7,4},{8,9},{9,10},{10,1... | collective-permute-start | bytes 2752520 | tf_op jit(solution)/shard_map/ppermute | solution.py:205
  20.9 29.5 %collective-permute-start.5 = (f32[32,7168]{1,0:T(8,128)S(1)}, f32[32,7168]{1,0:T(8,128)S(1)}, u32[]{:S(2)}, u32[]{:S(2)}) collective-permute-start(f32[32,7168]{1,0:T(8,128)S(1)} %get-tuple-element.16), channel_id=1, source_target_pairs={{0,3},{1,0},{2,1},{3,2},{4,7},{5,4},{6,5},{7,6},{8,11},{9,8},{10,9... | collective-permute-start | bytes 2752520 | tf_op jit(solution)/shard_map/ppermute | solution.py:209
  25.8 34.4 %collective-permute-start.10 = (f32[32,5376]{1,0:T(8,128)S(1)}, f32[32,5376]{1,0:T(8,128)S(1)}, u32[]{:S(2)}, u32[]{:S(2)}) collective-permute-start(f32[32,5376]{1,0:T(8,128)S(1)} %collective-permute-done.3.refs_1_), channel_id=1, source_target_pairs={{0,3},{1,0},{2,1},{3,2},{4,7},{5,4},{6,5},{7,6},{8,11},{9,8},{10,9... | collective-permute-start | bytes 2064392 | tf_op jit(solution)/shard_map/ppermute | solution.py:209
  29.2 31.2 %collective-permute-start.9 = (f32[32,5376]{1,0:T(8,128)S(1)}, f32[32,5376]{1,0:T(8,128)S(1)}, u32[]{:S(2)}, u32[]{:S(2)}) collective-permute-start(f32[32,5376]{1,0:T(8,128)S(1)} %collective-permute-done.2.refs_0_), channel_id=1, source_target_pairs={{0,1},{1,2},{2,3},{3,0},{4,5},{5,6},{6,7},{7,4},{8,9},{9,10},{10,1... | collective-permute-start | bytes 2064392 | tf_op jit(solution)/shard_map/ppermute | solution.py:205
  29.2 34.6 %collective-permute-start.7 = (f32[32,1792]{1,0:T(8,128)S(1)}, f32[32,1792]{1,0:T(8,128)S(1)}, u32[]{:S(2)}, u32[]{:S(2)}) collective-permute-start(f32[32,1792]{1,0:T(8,128)S(1)} %collective-permute-done.refs_4_.refs_0_), channel_id=1, source_target_pairs={{0,1},{1,2},{2,3},{3,0},{4,5},{5,6},{6,7},{7,4},{8,9},{9,10},{10,1... | collective-permute-start | bytes 688136 | tf_op jit(solution)/shard_map/ppermute | solution.py:205
  45.6 18.2 %collective-permute-start.8 = (f32[32,1792]{1,0:T(8,128)S(1)}, f32[32,1792]{1,0:T(8,128)S(1)}, u32[]{:S(2)}, u32[]{:S(2)}) collective-permute-start(f32[32,1792]{1,0:T(8,128)S(1)} %collective-permute-done.1.refs_5_.refs_1_), channel_id=1, source_target_pairs={{0,3},{1,0},{2,1},{3,2},{4,7},{5,4},{6,5},{7,6},{8,11},{9,8},{10,9... | collective-permute-start | bytes 688136 | tf_op jit(solution)/shard_map/ppermute | solution.py:209
  54.0 1.5 %collective-permute-start.6 = (f32[32,4,384]{2,1,0:T(4,128)S(1)}, f32[32,4,384]{2,1,0:T(4,128)S(1)}, u32[]{:S(2)}, u32[]{:S(2)}) collective-permute-start(f32[32,4,384]{2,1,0:T(4,128)S(1)} %get-tuple-element.18), channel_id=1, source_target_pairs={{0,4},{4,0},{8,12},{12,8},{16,20},{20,16},{24,28},{28,24},{32,36},... | collective-permute-start | bytes 589832 | tf_op jit(solution)/shard_map/ppermute | solution.py:213
  63.0 16.2 %copy-start.5 = (s32[384]{0:T(512)S(1)}, s32[384]{0:T(512)}, u32[]{:S(2)}) copy-start(s32[384]{0:T(512)} %param.10) | copy-start | bytes 4612
  63.0 16.2 %copy-start.6 = (s32[384]{0:T(512)S(1)}, s32[384]{0:T(512)}, u32[]{:S(2)}) copy-start(s32[384]{0:T(512)} %param.11) | copy-start | bytes 4612
  64.8 1.3 %collective-permute-start.11 = (f32[8,4,384]{2,1,0:T(4,128)S(1)}, f32[8,4,384]{2,1,0:T(4,128)S(1)}, u32[]{:S(2)}, u32[]{:S(2)}) collective-permute-start(f32[8,4,384]{2,1,0:T(4,128)S(1)} %get-tuple-element.20), channel_id=1, source_target_pairs={{0,4},{4,0},{8,12},{12,8},{16,20},{20,16},{24,28},{28,24},{32,36},... | collective-permute-start | bytes 147464 | tf_op jit(solution)/shard_map/ppermute | solution.py:213
  66.8 18.6 %all-to-all-start = ((f32[32,4,384]{2,1,0:T(4,128)}), f32[32,4,384]{2,1,0:T(4,128)S(1)}, u32[]{:S(2)}, u32[]{:S(2)}) async-start(f32[32,4,384]{2,1,0:T(4,128)} %shard_map.73), calls=%async_computation | async-start | bytes 393216 | tf_op jit(solution)/shard_map/all_to_all | solution.py:244

commit v6 on v4

--- a/solution.py
+++ b/solution.py
@@ -10,7 +10,7 @@
 F32 = jnp.float32
 BF16 = jnp.bfloat16
 STEP = 1792
-VMEM = pltpu.CompilerParams(vmem_limit_bytes=24 * 2**20)
+VMEM = pltpu.CompilerParams(vmem_limit_bytes=32 * 2**20)
 FREE = pl.CostEstimate(flops=0, bytes_accessed=0, transcendentals=0)
 GROUPS, LAYERS, CORES = 4, 8, 2
 ORDER = (4, 5, 6, 7, 0, 1, 2, 3)

time: 87.3 us -> 87.3 us (level)
  no operation moved by 1% of the time
where the time goes in v6:
time: 87.3 us; the launch traced here: 86 us
  waiting for transfers between devices  35.1 us (40%)
  starting transfers between devices  27.5 us (32%)
  Pallas kernels  16.3 us (19%)
  local copies, waits for them, and re-layouts  6.74 us (8%)
    ppermute x5, waiting for transfers between devices, right(): return lax.ppermute(x, 'ab', [(i, (i + 1) % GROUPS) for i in range(GROUPS)])  17.3 us
    all_to_all x1, starting transfers between devices, local(): lax.all_to_all(part_sum, 'cd', 0, 0, tiled=True, axis_index_groups=planes)  12.4 us
    ppermute x5, starting transfers between devices, left(): return lax.ppermute(x, 'ab', [(i, (i - 1) % GROUPS) for i in range(GROUPS)])  10.9 us
    pallas_call x4, Pallas kernels, partial_sums(): pl.pallas_call(functools.partial(sum_kernel, slabs), grid=(pairs // STEP,...  9.63 us
    ppermute x5, waiting for transfers between devices, left(): return lax.ppermute(x, 'ab', [(i, (i - 1) % GROUPS) for i in range(GROUPS)])  8.95 us
    all_to_all x1, waiting for transfers between devices, local(): lax.all_to_all(part_sum, 'cd', 0, 0, tiled=True, axis_index_groups=planes)  6.24 us
    unnamed x14, local copies, waits for them, and re-layouts  5.65 us
    ppermute x5, starting transfers between devices, right(): return lax.ppermute(x, 'ab', [(i, (i + 1) % GROUPS) for i in range(GROUPS)])  3.91 us
  transfers between devices with their start and end apart: 13, of which 10 were waited for; matrix products, arithmetic and copies ran while one was open for 0% of the time, Pallas kernels for 16%

profile of v6, /device:TPU:32, one launch (start us, length us, event | category | flops | bytes accessed | tf_op | source)
XLA Modules:
  0.0 86.0 jit_solution(11256786600840724212)
XLA Ops:
  0.0 1.1 %slice_bitcast_fusion = (f32[32,1792]{1,0:T(8,128)S(1)}, f32[32,1792]{1,0:T(8,128)S(1)}) fusion(f32[2,32,7168]{2,1,0:T(8,128)} %own_ref.3), kind=kLoop, calls=%fused_computation | loop fusion | bytes 917504 | tf_op jit(solution)/shard_map/squeeze | solution.py:222
  1.1 1.6 %collective-permute-start = (f32[32,1792]{1,0:T(8,128)S(1)}, f32[32,1792]{1,0:T(8,128)S(1)}, u32[]{:S(2)}, u32[]{:S(2)}) collective-permute-start(f32[32,1792]{1,0:T(8,128)S(1)} %get-tuple-element.24), channel_id=1, source_target_pairs={{0,1},{1,2},{2,3},{3,0},{4,5},{5,6},{6,7},{7,4},{8,9},{9,10},{10,1... | collective-permute-start | bytes 688136 | tf_op jit(solution)/shard_map/ppermute | solution.py:204
  2.7 1.7 %collective-permute-start.1 = (f32[32,1792]{1,0:T(8,128)S(1)}, f32[32,1792]{1,0:T(8,128)S(1)}, u32[]{:S(2)}, u32[]{:S(2)}) collective-permute-start(f32[32,1792]{1,0:T(8,128)S(1)} %get-tuple-element.23), channel_id=1, source_target_pairs={{0,3},{1,0},{2,1},{3,2},{4,7},{5,4},{6,5},{7,6},{8,11},{9,8},{10,9... | collective-permute-start | bytes 688136 | tf_op jit(solution)/shard_map/ppermute | solution.py:208
  4.4 1.5 %copy-done.2 = f32[2,32,7168]{2,1,0:T(8,128)S(1)} copy-done((f32[2,32,7168]{2,1,0:T(8,128)S(1)}, f32[2,32,7168]{2,1,0:T(8,128)}, u32[]{:S(2)}) %copy-start.2) | copy-done | bytes 1835032
  5.9 0.4 shard_map.66
  6.3 0.4 collective-permute-start.2
  6.6 3.0 %collective-permute-start.3 = (f32[32,5376]{1,0:T(8,128)S(1)}, f32[32,5376]{1,0:T(8,128)S(1)}, u32[]{:S(2)}, u32[]{:S(2)}) collective-permute-start(f32[32,5376]{1,0:T(8,128)S(1)} %get-tuple-element.14), channel_id=1, source_target_pairs={{0,3},{1,0},{2,1},{3,2},{4,7},{5,4},{6,5},{7,6},{8,11},{9,8},{10,9... | collective-permute-start | bytes 2064392 | tf_op jit(solution)/shard_map/ppermute | solution.py:208
  9.7 0.3 collective-permute-done.refs_4_.refs_0_
  10.0 1.1 %collective-permute-done.1.refs_5_.refs_1_ = f32[32,1792]{1,0:T(8,128)S(1)} collective-permute-done((f32[32,1792]{1,0:T(8,128)S(1)}, f32[32,1792]{1,0:T(8,128)S(1)}, u32[]{:S(2)}, u32[]{:S(2)}) %collective-permute-start.1) | collective-permute-done | bytes 229408 | tf_op jit(solution)/shard_map/ppermute | solution.py:208
  11.1 4.1 %copy-done = f32[7168,384]{1,0:T(8,128)S(1)} copy-done((f32[7168,384]{1,0:T(8,128)S(1)}, f32[7168,384]{1,0:T(8,128)}, u32[]{:S(2)}) %copy-start) | copy-done | bytes 11010072
  15.2 3.5 %shard_map.64.refs_0_.own_ref = f32[64,384]{1,0:T(8,128)S(1)} custom-call(f32[2,32,7168]{2,1,0:T(8,128)S(1)} %copy-done.2, f32[2,32,7168]{2,1,0:T(8,128)S(1)} %copy-done.2, f32[2,7168]{1,0:T(2,128)S(1)} %pad_maximum_fusion.refs_2_, f32[7168,384]{1,0:T(8,128)S(1)} %copy-done, f32[32,1792]{1,0:T(8,128)S(1)} %collective-permute-done.refs_4_.refs_0_, ...), custom_call_target="tpu_custom_call" | custom-call | tf_op jit(solution)/shard_map/pallas_call | solution.py:60
  18.7 0.5 shard_map.68
  19.2 1.7 %collective-permute-start.4 = (f32[32,7168]{1,0:T(8,128)S(1)}, f32[32,7168]{1,0:T(8,128)S(1)}, u32[]{:S(2)}, u32[]{:S(2)}) collective-permute-start(f32[32,7168]{1,0:T(8,128)S(1)} %get-tuple-element.15), channel_id=1, source_target_pairs={{0,1},{1,2},{2,3},{3,0},{4,5},{5,6},{6,7},{7,4},{8,9},{9,10},{10,1... | collective-permute-start | bytes 2752520 | tf_op jit(solution)/shard_map/ppermute | solution.py:204
  20.9 1.6 %collective-permute-start.5 = (f32[32,7168]{1,0:T(8,128)S(1)}, f32[32,7168]{1,0:T(8,128)S(1)}, u32[]{:S(2)}, u32[]{:S(2)}) collective-permute-start(f32[32,7168]{1,0:T(8,128)S(1)} %get-tuple-element.16), channel_id=1, source_target_pairs={{0,3},{1,0},{2,1},{3,2},{4,7},{5,4},{6,5},{7,6},{8,11},{9,8},{10,9... | collective-permute-start | bytes 2752520 | tf_op jit(solution)/shard_map/ppermute | solution.py:208
  22.5 3.3 %collective-permute-done.3.refs_1_ = f32[32,5376]{1,0:T(8,128)S(1)} collective-permute-done((f32[32,5376]{1,0:T(8,128)S(1)}, f32[32,5376]{1,0:T(8,128)S(1)}, u32[]{:S(2)}, u32[]{:S(2)}) %collective-permute-start.3) | collective-permute-done | bytes 688160 | tf_op jit(solution)/shard_map/ppermute | solution.py:208
  25.8 3.3 %collective-permute-start.10 = (f32[32,5376]{1,0:T(8,128)S(1)}, f32[32,5376]{1,0:T(8,128)S(1)}, u32[]{:S(2)}, u32[]{:S(2)}) collective-permute-start(f32[32,5376]{1,0:T(8,128)S(1)} %collective-permute-done.3.refs_1_), channel_id=1, source_target_pairs={{0,3},{1,0},{2,1},{3,2},{4,7},{5,4},{6,5},{7,6},{8,11},{9,8},{10,9... | collective-permute-start | bytes 2064392 | tf_op jit(solution)/shard_map/ppermute | solution.py:208
  29.2 0.3 collective-permute-start.7
  29.5 16.1 %collective-permute-done.4.refs_0_ = f32[32,7168]{1,0:T(8,128)S(1)} collective-permute-done((f32[32,7168]{1,0:T(8,128)S(1)}, f32[32,7168]{1,0:T(8,128)S(1)}, u32[]{:S(2)}, u32[]{:S(2)}) %collective-permute-start.4) | collective-permute-done | bytes 917536 | tf_op jit(solution)/shard_map/ppermute | solution.py:204
  45.6 1.2 %collective-permute-start.8 = (f32[32,1792]{1,0:T(8,128)S(1)}, f32[32,1792]{1,0:T(8,128)S(1)}, u32[]{:S(2)}, u32[]{:S(2)}) collective-permute-start(f32[32,1792]{1,0:T(8,128)S(1)} %collective-permute-done.1.refs_5_.refs_1_), channel_id=1, source_target_pairs={{0,3},{1,0},{2,1},{3,2},{4,7},{5,4},{6,5},{7,6},{8,11},{9,8},{10,9... | collective-permute-start | bytes 688136 | tf_op jit(solution)/shard_map/ppermute | solution.py:208
  46.8 0.8 shard_map.65
  47.7 2.7 %shard_map.67 = f32[64,384]{1,0:T(8,128)S(1)} custom-call(f32[32,5376]{1,0:T(8,128)S(1)} %collective-permute-done.2.refs_0_, f32[32,5376]{1,0:T(8,128)S(1)} %collective-permute-done.3.refs_1_, f32[2,7168]{1,0:T(2,128)S(1)} %pad_maximum_fusion.refs_2_, f32[7168,384]{1,0:T(8,128)S(1)} %copy-done.1), custom_call_target="tpu_custom_call" | custom-call | tf_op jit(solution)/shard_map/pallas_call | solution.py:74
  50.4 3.5 %shard_map.69.far_ref = f32[64,384]{1,0:T(8,128)S(1)} custom-call(f32[32,7168]{1,0:T(8,128)S(1)} %collective-permute-done.4.refs_0_, f32[32,7168]{1,0:T(8,128)S(1)} %collective-permute-done.5.refs_1_, f32[2,7168]{1,0:T(2,128)S(1)} %pad_maximum_fusion.refs_2_, f32[7168,384]{1,0:T(8,128)S(1)} %copy-done.1), custom_call_target="tpu_custom_call" | custom-call | tf_op jit(solution)/shard_map/pallas_call | solution.py:74
  54.3 1.4 %collective-permute-done.6.refs_4_.got_ref = f32[32,4,384]{2,1,0:T(4,128)S(1)} collective-permute-done((f32[32,4,384]{2,1,0:T(4,128)S(1)}, f32[32,4,384]{2,1,0:T(4,128)S(1)}, u32[]{:S(2)}, u32[]{:S(2)}) %collective-permute-start.6) | collective-permute-done | bytes 196640 | tf_op jit(solution)/shard_map/ppermute | solution.py:212
  55.7 4.5 %collective-permute-done.10.refs_1_ = f32[32,5376]{1,0:T(8,128)S(1)} collective-permute-done((f32[32,5376]{1,0:T(8,128)S(1)}, f32[32,5376]{1,0:T(8,128)S(1)}, u32[]{:S(2)}, u32[]{:S(2)}) %collective-permute-start.10) | collective-permute-done | bytes 688160 | tf_op jit(solution)/shard_map/ppermute | solution.py:208
  60.3 2.6 %shard_map.71.refs_4_ = f32[64,384]{1,0:T(8,128)S(1)} custom-call(f32[32,5376]{1,0:T(8,128)S(1)} %collective-permute-done.9.refs_0_, f32[32,5376]{1,0:T(8,128)S(1)} %collective-permute-done.10.refs_1_, f32[2,7168]{1,0:T(2,128)S(1)} %pad_maximum_fusion.refs_2_, f32[7168,384]{1,0:T(8,128)S(1)} %copy-done.1, ...), custom_call_target="tpu_custom_call" | custom-call | tf_op jit(solution)/shard_map/pallas_call | solution.py:74
  63.0 0.8 collective-permute-done.7.refs_0_
  63.8 0.9 %shard_map.72 = (f32[8,4,384]{2,1,0:T(4,128)S(1)}, f32[8,4,384]{2,1,0:T(4,128)S(1)}) custom-call(f32[32,1792]{1,0:T(8,128)S(1)} %collective-permute-done.7.refs_0_, f32[32,1792]{1,0:T(8,128)S(1)} %collective-permute-done.8.refs_1_, f32[2,7168]{1,0:T(2,128)S(1)} %pad_maximum_fusion.refs_2_, f32[7168,384]{1,0:T(8,128)S(1)} %copy-done.1, ...), custom_call_target="tpu_custom_call" | custom-call | tf_op jit(solution)/shard_map/pallas_call | solution.py:148
  64.8 1.2 %collective-permute-done.11.got_opposite_ref = f32[8,4,384]{2,1,0:T(4,128)S(1)} collective-permute-done((f32[8,4,384]{2,1,0:T(4,128)S(1)}, f32[8,4,384]{2,1,0:T(4,128)S(1)}, u32[]{:S(2)}, u32[]{:S(2)}) %collective-permute-start.11) | collective-permute-done | bytes 49184 | tf_op jit(solution)/shard_map/ppermute | solution.py:212
  66.0 0.7 shard_map.73
  66.7 12.4 %all-to-all-start = ((f32[32,4,384]{2,1,0:T(4,128)}), f32[32,4,384]{2,1,0:T(4,128)S(1)}, u32[]{:S(2)}, u32[]{:S(2)}) async-start(f32[32,4,384]{2,1,0:T(4,128)} %shard_map.73), calls=%async_computation | async-start | bytes 393216 | tf_op jit(solution)/shard_map/all_to_all | solution.py:243
  79.1 6.2 %all-to-all-done.shares_ref = f32[32,4,384]{2,1,0:T(4,128)S(1)} async-done(((f32[32,4,384]{2,1,0:T(4,128)}), f32[32,4,384]{2,1,0:T(4,128)S(1)}, u32[]{:S(2)}, u32[]{:S(2)}) %all-to-all-start) | async-done | bytes 196640 | tf_op jit(solution)/shard_map/all_to_all | solution.py:243
  85.3 0.6 shard_map.74
  (26 shorter events, 0.7 us)
Async XLA Ops:
  0.0 9.6 %copy-start.3 = (s32[7168]{0:T(1024)S(1)}, s32[7168]{0:T(1024)}, u32[]{:S(2)}) copy-start(s32[7168]{0:T(1024)} %param.8) | copy-start | bytes 86020
  0.0 9.6 %copy-start.4 = (s32[7168]{0:T(1024)S(1)}, s32[7168]{0:T(1024)}, u32[]{:S(2)}) copy-start(s32[7168]{0:T(1024)} %param.9) | copy-start | bytes 86020
  1.1 8.9 %collective-permute-start = (f32[32,1792]{1,0:T(8,128)S(1)}, f32[32,1792]{1,0:T(8,128)S(1)}, u32[]{:S(2)}, u32[]{:S(2)}) collective-permute-start(f32[32,1792]{1,0:T(8,128)S(1)} %get-tuple-element.24), channel_id=1, source_target_pairs={{0,1},{1,2},{2,3},{3,0},{4,5},{5,6},{6,7},{7,4},{8,9},{9,10},{10,1... | collective-permute-start | bytes 688136 | tf_op jit(solution)/shard_map/ppermute | solution.py:204
  2.7 8.4 %collective-permute-start.1 = (f32[32,1792]{1,0:T(8,128)S(1)}, f32[32,1792]{1,0:T(8,128)S(1)}, u32[]{:S(2)}, u32[]{:S(2)}) collective-permute-start(f32[32,1792]{1,0:T(8,128)S(1)} %get-tuple-element.23), channel_id=1, source_target_pairs={{0,3},{1,0},{2,1},{3,2},{4,7},{5,4},{6,5},{7,6},{8,11},{9,8},{10,9... | collective-permute-start | bytes 688136 | tf_op jit(solution)/shard_map/ppermute | solution.py:208
  4.4 1.5 %copy-start.2 = (f32[2,32,7168]{2,1,0:T(8,128)S(1)}, f32[2,32,7168]{2,1,0:T(8,128)}, u32[]{:S(2)}) copy-start(f32[2,32,7168]{2,1,0:T(8,128)} %own_ref.3) | copy-start | bytes 5505028
  6.3 22.9 %collective-permute-start.2 = (f32[32,5376]{1,0:T(8,128)S(1)}, f32[32,5376]{1,0:T(8,128)S(1)}, u32[]{:S(2)}, u32[]{:S(2)}) collective-permute-start(f32[32,5376]{1,0:T(8,128)S(1)} %get-tuple-element.13), channel_id=1, source_target_pairs={{0,1},{1,2},{2,3},{3,0},{4,5},{5,6},{6,7},{7,4},{8,9},{9,10},{10,1... | collective-permute-start | bytes 2064392 | tf_op jit(solution)/shard_map/ppermute | solution.py:204
  6.6 19.2 %collective-permute-start.3 = (f32[32,5376]{1,0:T(8,128)S(1)}, f32[32,5376]{1,0:T(8,128)S(1)}, u32[]{:S(2)}, u32[]{:S(2)}) collective-permute-start(f32[32,5376]{1,0:T(8,128)S(1)} %get-tuple-element.14), channel_id=1, source_target_pairs={{0,3},{1,0},{2,1},{3,2},{4,7},{5,4},{6,5},{7,6},{8,11},{9,8},{10,9... | collective-permute-start | bytes 2064392 | tf_op jit(solution)/shard_map/ppermute | solution.py:208
  11.1 4.1 %copy-start = (f32[7168,384]{1,0:T(8,128)S(1)}, f32[7168,384]{1,0:T(8,128)}, u32[]{:S(2)}) copy-start(f32[7168,384]{1,0:T(8,128)} %refs_3_.11) | copy-start | bytes 33030148
  15.2 31.6 %copy-start.1 = (f32[7168,384]{1,0:T(8,128)S(1)}, f32[7168,384]{1,0:T(8,128)}, u32[]{:S(2)}) copy-start(f32[7168,384]{1,0:T(8,128)} %refs_3_.11) | copy-start | bytes 33030148
  19.2 26.4 %collective-permute-start.4 = (f32[32,7168]{1,0:T(8,128)S(1)}, f32[32,7168]{1,0:T(8,128)S(1)}, u32[]{:S(2)}, u32[]{:S(2)}) collective-permute-start(f32[32,7168]{1,0:T(8,128)S(1)} %get-tuple-element.15), channel_id=1, source_target_pairs={{0,1},{1,2},{2,3},{3,0},{4,5},{5,6},{6,7},{7,4},{8,9},{9,10},{10,1... | collective-permute-start | bytes 2752520 | tf_op jit(solution)/shard_map/ppermute | solution.py:204
  20.9 29.4 %collective-permute-start.5 = (f32[32,7168]{1,0:T(8,128)S(1)}, f32[32,7168]{1,0:T(8,128)S(1)}, u32[]{:S(2)}, u32[]{:S(2)}) collective-permute-start(f32[32,7168]{1,0:T(8,128)S(1)} %get-tuple-element.16), channel_id=1, source_target_pairs={{0,3},{1,0},{2,1},{3,2},{4,7},{5,4},{6,5},{7,6},{8,11},{9,8},{10,9... | collective-permute-start | bytes 2752520 | tf_op jit(solution)/shard_map/ppermute | solution.py:208
  25.8 34.4 %collective-permute-start.10 = (f32[32,5376]{1,0:T(8,128)S(1)}, f32[32,5376]{1,0:T(8,128)S(1)}, u32[]{:S(2)}, u32[]{:S(2)}) collective-permute-start(f32[32,5376]{1,0:T(8,128)S(1)} %collective-permute-done.3.refs_1_), channel_id=1, source_target_pairs={{0,3},{1,0},{2,1},{3,2},{4,7},{5,4},{6,5},{7,6},{8,11},{9,8},{10,9... | collective-permute-start | bytes 2064392 | tf_op jit(solution)/shard_map/ppermute | solution.py:208
  29.2 31.2 %collective-permute-start.9 = (f32[32,5376]{1,0:T(8,128)S(1)}, f32[32,5376]{1,0:T(8,128)S(1)}, u32[]{:S(2)}, u32[]{:S(2)}) collective-permute-start(f32[32,5376]{1,0:T(8,128)S(1)} %collective-permute-done.2.refs_0_), channel_id=1, source_target_pairs={{0,1},{1,2},{2,3},{3,0},{4,5},{5,6},{6,7},{7,4},{8,9},{9,10},{10,1... | collective-permute-start | bytes 2064392 | tf_op jit(solution)/shard_map/ppermute | solution.py:204
  29.2 34.6 %collective-permute-start.7 = (f32[32,1792]{1,0:T(8,128)S(1)}, f32[32,1792]{1,0:T(8,128)S(1)}, u32[]{:S(2)}, u32[]{:S(2)}) collective-permute-start(f32[32,1792]{1,0:T(8,128)S(1)} %collective-permute-done.refs_4_.refs_0_), channel_id=1, source_target_pairs={{0,1},{1,2},{2,3},{3,0},{4,5},{5,6},{6,7},{7,4},{8,9},{9,10},{10,1... | collective-permute-start | bytes 688136 | tf_op jit(solution)/shard_map/ppermute | solution.py:204
  45.6 18.2 %collective-permute-start.8 = (f32[32,1792]{1,0:T(8,128)S(1)}, f32[32,1792]{1,0:T(8,128)S(1)}, u32[]{:S(2)}, u32[]{:S(2)}) collective-permute-start(f32[32,1792]{1,0:T(8,128)S(1)} %collective-permute-done.1.refs_5_.refs_1_), channel_id=1, source_target_pairs={{0,3},{1,0},{2,1},{3,2},{4,7},{5,4},{6,5},{7,6},{8,11},{9,8},{10,9... | collective-permute-start | bytes 688136 | tf_op jit(solution)/shard_map/ppermute | solution.py:208
  54.0 1.7 %collective-permute-start.6 = (f32[32,4,384]{2,1,0:T(4,128)S(1)}, f32[32,4,384]{2,1,0:T(4,128)S(1)}, u32[]{:S(2)}, u32[]{:S(2)}) collective-permute-start(f32[32,4,384]{2,1,0:T(4,128)S(1)} %get-tuple-element.18), channel_id=1, source_target_pairs={{0,4},{4,0},{8,12},{12,8},{16,20},{20,16},{24,28},{28,24},{32,36},... | collective-permute-start | bytes 589832 | tf_op jit(solution)/shard_map/ppermute | solution.py:212
  63.0 16.1 %copy-start.5 = (s32[384]{0:T(512)S(1)}, s32[384]{0:T(512)}, u32[]{:S(2)}) copy-start(s32[384]{0:T(512)} %param.10) | copy-start | bytes 4612
  63.0 16.1 %copy-start.6 = (s32[384]{0:T(512)S(1)}, s32[384]{0:T(512)}, u32[]{:S(2)}) copy-start(s32[384]{0:T(512)} %param.11) | copy-start | bytes 4612
  64.7 1.3 %collective-permute-start.11 = (f32[8,4,384]{2,1,0:T(4,128)S(1)}, f32[8,4,384]{2,1,0:T(4,128)S(1)}, u32[]{:S(2)}, u32[]{:S(2)}) collective-permute-start(f32[8,4,384]{2,1,0:T(4,128)S(1)} %get-tuple-element.20), channel_id=1, source_target_pairs={{0,4},{4,0},{8,12},{12,8},{16,20},{20,16},{24,28},{28,24},{32,36},... | collective-permute-start | bytes 147464 | tf_op jit(solution)/shard_map/ppermute | solution.py:212
  66.7 18.6 %all-to-all-start = ((f32[32,4,384]{2,1,0:T(4,128)}), f32[32,4,384]{2,1,0:T(4,128)S(1)}, u32[]{:S(2)}, u32[]{:S(2)}) async-start(f32[32,4,384]{2,1,0:T(4,128)} %shard_map.73), calls=%async_computation | async-start | bytes 393216 | tf_op jit(solution)/shard_map/all_to_all | solution.py:243
